TPU v7x, 256 devices: a whole 4x4x8 slice. The times are simulated.
256 devices in a mesh: shard: 128 (over z, x, y), mp: 2 (over core).
Axes of the slice: x: 4, y: 4, z: 8, core: 2. Of those that a mesh axis runs over, the one named last changes fastest.
Arguments:
- item_rows: float32 [32768, 256], P('shard', 'mp'), may hold values from -6 to 6
- first_moment: float32 [32768, 256], P('shard', 'mp'), may hold values from -2 to 2
- second_moment: float32 [32768, 256], P('shard', 'mp'), may hold values from 0.01 to 4
- item_cot: bfloat16 [32768, 256], P('shard', 'mp'), may hold values from -6 to 6
- tile_bits: int32 [2048, 8, 128], P('shard'), may hold values from 0 to 65535, as said below
- tile_item: int32 [2048], P('shard'), may hold values from 0 to 1
- tile_dest: int32 [2048], P('shard'), may hold values from 0 to 127
- basket_gain: float32 [256], replicated, may hold values from 0.1 to 1.9
- item_gain: float32 [256], replicated, may hold values from 0.1 to 1.9
- gate_basket: bfloat16 [256, 2048], P(None, 'mp'), may hold values from -0.375 to 0.375
- up_basket: bfloat16 [256, 2048], P(None, 'mp'), may hold values from -0.375 to 0.375
- down_basket: bfloat16 [2048, 256], P('mp'), may hold values from -0.125 to 0.125
- gate_item: bfloat16 [256, 2048], P(None, 'mp'), may hold values from -0.375 to 0.375
- up_item: bfloat16 [256, 2048], P(None, 'mp'), may hold values from -0.375 to 0.375
- down_item: bfloat16 [2048, 256], P('mp'), may hold values from -0.125 to 0.125
Outputs:
- new_rows: float32 [32768, 256], P('shard', 'mp')
- new_first: float32 [32768, 256], P('shard', 'mp')
- new_second: float32 [32768, 256], P('shard', 'mp')
Inputs may be any that keep to these rules, and one draw needn't show every extreme that they name: `tile_bits`: each word holds 16 independent incidence bits in its low bits.
All inputs are finite; a program needn't handle non-finite values.
Results may differ from a plain program's by a relative error of at most 0.007.
Values may be sent and summed in bfloat16 or wider, within the bound.
A program may use at most 128 MiB of HBM per device.

v0:
```python
import jax
import jax.numpy as jnp
from jax import lax
from jax.sharding import Mesh
from jax.sharding import PartitionSpec as P

D = 256
BLOCK = 128
SHARD = ("shard_0", "shard_1", "shard_2")


NORM_EPSILON = 1e-05
LEARNING_RATE = 0.01
BETA_FIRST = 0.9
BETA_SECOND = 0.99
ADAM_EPSILON = 1e-08


def gather_axes(value, axes, dim):
    for axis in reversed(axes):
        value = lax.all_gather(value, axis, axis=dim, tiled=True)
    return value


def sent_to_all(value, axis):
    copies = jnp.broadcast_to(value, (lax.axis_size(axis), *value.shape))
    return lax.all_to_all(copies, axis, split_axis=0, concat_axis=0, tiled=True)


def laid_out(pieces, dim):
    pieces = jnp.moveaxis(pieces, 0, dim)
    dims = pieces.shape
    return pieces.reshape(*dims[:dim], dims[dim] * dims[dim + 1], *dims[dim + 2 :])


def gather_directly(value, axis, dim):
    pieces = sent_to_all(value, axis)
    return laid_out(pieces, dim)


def cut_along(value, dim, count):
    dims = value.shape
    pieces = value.reshape(*dims[:dim], count, dims[dim] // count, *dims[dim + 1 :])
    return jnp.moveaxis(pieces, dim, 0)


def sum_at_owner(value, axis, dim):
    count = lax.axis_size(axis)
    pieces = lax.all_to_all(cut_along(value, dim, count), axis, 0, 0, tiled=True)
    return jnp.sum(pieces.astype(jnp.float32), axis=0)


def over_copies(value, axis):
    return sent_to_all(value, axis).astype(jnp.float32).sum(axis=0)


def unpack_tiles(packed):
    shifts = jnp.arange(16, dtype=jnp.int32)
    bit_values = jnp.right_shift(packed[:, :, None, :], shifts[None, None, :, None]) & 1
    return bit_values.reshape(packed.shape[0], packed.shape[1] * 16, packed.shape[2]).astype(
        jnp.bfloat16
    )


def silu_parts(gate_values):
    sigmoid = jax.nn.sigmoid(gate_values)
    return (gate_values * sigmoid, sigmoid * (1.0 + gate_values * (1.0 - sigmoid)))


def rms_scale(values):
    return lax.rsqrt(jnp.mean(values * values, axis=-1, keepdims=True) + NORM_EPSILON)


def owner_sums(partials, tile_dest):
    block_total = lax.axis_size(SHARD)
    coalesced = jax.ops.segment_sum(partials, tile_dest, num_segments=block_total)
    received = lax.all_to_all(
        coalesced.astype(jnp.bfloat16), SHARD, split_axis=0, concat_axis=0, tiled=True
    ).astype(coalesced.dtype)
    return jnp.sum(received, axis=0)


def spread_items(owned, masks, tile_item, tile_dest, item_blocks):
    gathered = gather_axes(owned, SHARD, 0)
    gathered = gathered.reshape(-1, BLOCK, owned.shape[1])
    selected = jnp.take(gathered, tile_dest, axis=0)
    contrib = jnp.einsum("tib,tbf->tif", masks, selected, preferred_element_type=jnp.float32)
    summed = jax.ops.segment_sum(contrib, tile_item, num_segments=item_blocks)
    return summed.reshape(item_blocks * BLOCK, owned.shape[1])


def whole_features(values):
    return gather_directly(values.astype(jnp.bfloat16), "mp", 1).astype(values.dtype)


def local(
    item_rows,
    first_moment,
    second_moment,
    item_cot,
    tile_bits,
    tile_item,
    tile_dest,
    basket_gain,
    item_gain,
    gate_basket,
    up_basket,
    down_basket,
    gate_item,
    up_item,
    down_item,
):
    half_width = item_rows.shape[1]
    item_blocks = item_rows.shape[0] // BLOCK
    offset = lax.axis_index("mp") * half_width
    masks = unpack_tiles(tile_bits)
    rows_blocks = item_rows.astype(jnp.bfloat16).reshape(item_blocks, BLOCK, half_width)
    picked = jnp.take(rows_blocks, tile_item, axis=0)
    partials = jnp.einsum("tib,tif->tbf", masks, picked, preferred_element_type=jnp.float32)
    basket_sum = owner_sums(partials, tile_dest)
    sum_full = whole_features(basket_sum)
    scale_basket = rms_scale(sum_full)
    normed = sum_full * scale_basket * basket_gain
    normed_bf = normed.astype(jnp.bfloat16)
    gate_pre = jnp.dot(normed_bf, gate_basket, preferred_element_type=jnp.float32)
    up_pre = jnp.dot(normed_bf, up_basket, preferred_element_type=jnp.float32)
    silu_value, silu_slope = silu_parts(gate_pre)
    hidden = (silu_value * up_pre).astype(jnp.bfloat16)
    down_part = jnp.dot(hidden, down_basket, preferred_element_type=jnp.float32)
    down_mine = sum_at_owner(down_part.astype(jnp.bfloat16), "mp", 1)
    basket_out = (lax.dynamic_slice_in_dim(normed, offset, half_width, 1) + down_mine).astype(
        jnp.bfloat16
    )
    message = spread_items(basket_out, masks, tile_item, tile_dest, item_blocks)
    message_full = gather_directly(message, "mp", 1)
    scale_item = rms_scale(message_full)
    query = (message_full * scale_item * item_gain).astype(jnp.bfloat16)
    gate_item_pre = jnp.dot(query, gate_item, preferred_element_type=jnp.float32)
    up_item_pre = jnp.dot(query, up_item, preferred_element_type=jnp.float32)
    item_value, item_slope = silu_parts(gate_item_pre)
    cot_full = gather_directly(item_cot, "mp", 1)
    grad_hidden = jnp.einsum("rd,hd->rh", cot_full, down_item, preferred_element_type=jnp.float32)
    grad_up = (grad_hidden * item_value).astype(jnp.bfloat16)
    grad_gate = (grad_hidden * up_item_pre * item_slope).astype(jnp.bfloat16)
    query_part = jnp.einsum(
        "rh,dh->rd", grad_gate, gate_item, preferred_element_type=jnp.float32
    ) + jnp.einsum("rh,dh->rd", grad_up, up_item, preferred_element_type=jnp.float32)
    gain_mine = lax.dynamic_slice_in_dim(item_gain, offset, half_width, 0)
    query_full = over_copies(query_part.astype(jnp.bfloat16), "mp").astype(jnp.float32)
    inner = jnp.sum(item_gain * query_full * message_full, axis=1, keepdims=True)
    grad_query = lax.dynamic_slice_in_dim(query_full, offset, half_width, 1)
    cubed_item = scale_item * scale_item * scale_item
    grad_message = (scale_item * gain_mine * grad_query - message * cubed_item * inner / D).astype(
        jnp.bfloat16
    )
    grad_blocks = grad_message.reshape(item_blocks, BLOCK, half_width)
    grad_picked = jnp.take(grad_blocks, tile_item, axis=0)
    grad_partials = jnp.einsum(
        "tib,tif->tbf", masks, grad_picked, preferred_element_type=jnp.float32
    )
    grad_out = owner_sums(grad_partials, tile_dest)
    grad_out_full = whole_features(grad_out)
    grad_out_bf = grad_out_full.astype(jnp.bfloat16)
    grad_basket_hidden = jnp.einsum(
        "bd,hd->bh", grad_out_bf, down_basket, preferred_element_type=jnp.float32
    )
    grad_basket_up = (grad_basket_hidden * silu_value).astype(jnp.bfloat16)
    grad_basket_gate = (grad_basket_hidden * up_pre * silu_slope).astype(jnp.bfloat16)
    normed_part = jnp.einsum(
        "bh,dh->bd", grad_basket_gate, gate_basket, preferred_element_type=jnp.float32
    ) + jnp.einsum("bh,dh->bd", grad_basket_up, up_basket, preferred_element_type=jnp.float32)
    grad_normed = grad_out_full + over_copies(normed_part.astype(jnp.bfloat16), "mp").astype(
        jnp.float32
    )
    inner_basket = jnp.sum(basket_gain * grad_normed * sum_full, axis=1, keepdims=True)
    cubed_basket = scale_basket * scale_basket * scale_basket
    grad_sum = scale_basket * basket_gain * grad_normed - sum_full * cubed_basket * inner_basket / D
    grad_sum_mine = lax.dynamic_slice_in_dim(grad_sum, offset, half_width, 1).astype(jnp.bfloat16)
    back_items = spread_items(grad_sum_mine, masks, tile_item, tile_dest, item_blocks)
    gradient = item_cot.astype(jnp.float32) + back_items
    new_first = BETA_FIRST * first_moment + (1.0 - BETA_FIRST) * gradient
    new_second = BETA_SECOND * second_moment + (1.0 - BETA_SECOND) * gradient * gradient
    new_rows = item_rows - LEARNING_RATE * new_first / (jnp.sqrt(new_second) + ADAM_EPSILON)
    return (new_rows, new_first, new_second)


def solution(mesh):
    finer = Mesh(
        mesh.devices.reshape(8, 4, 4, mesh.shape["mp"]), ("shard_0", "shard_1", "shard_2", "mp")
    )
    return jax.shard_map(
        local,
        mesh=finer,
        in_specs=(
            P(SHARD, "mp"),
            P(SHARD, "mp"),
            P(SHARD, "mp"),
            P(SHARD, "mp"),
            P(SHARD, None, None),
            P(SHARD),
            P(SHARD),
            P(),
            P(),
            P(None, "mp"),
            P(None, "mp"),
            P("mp", None),
            P(None, "mp"),
            P(None, "mp"),
            P("mp", None),
        ),
        out_specs=(P(SHARD, "mp"), P(SHARD, "mp"), P(SHARD, "mp")),
        check_vma=False,
    )
```

profile of v0, /device:TPU:1, one launch (start us, length us, event | category | flops | bytes accessed | tf_op | source)
XLA Modules:
  0.0 473.7 jit_solution(1845550905373578046)
XLA Ops:
  11.7 4.3 broadcast.92.clone
  16.0 3.3 scatter_fusion
  19.3 6.3 %convert_element_type.91 = bf16[128,128,128]{2,1,0:T(8,128)(2,1)} convert(f32[128,128,128]{2,1,0:T(8,128)} %scatter_fusion) | non-fusion elementwise | flops 2097152 | bytes 12582912 | tf_op jit(solution)/shard_map/convert_element_type | solution.py:78
  25.7 17.0 %all-to-all-start = ((bf16[128,128,128]{2,1,0:T(8,128)(2,1)}), bf16[128,128,128]{2,1,0:T(8,128)(2,1)}, u32[]{:S(2)}, u32[]{:S(2)}) async-start(bf16[128,128,128]{2,1,0:T(8,128)(2,1)} %convert_element_type.91), calls=%async_computation | async-start | bytes 8388608 | tf_op jit(solution)/shard_map/all_to_all | solution.py:77
  42.7 93.2 %all-to-all-done = bf16[128,128,128]{2,1,0:T(8,128)(2,1)} async-done(((bf16[128,128,128]{2,1,0:T(8,128)(2,1)}), bf16[128,128,128]{2,1,0:T(8,128)(2,1)}, u32[]{:S(2)}, u32[]{:S(2)}) %all-to-all-start) | async-done | bytes 4194336 | tf_op jit(solution)/shard_map/all_to_all | solution.py:77
  135.9 2.8 reduce_sum.91
  138.9 6.8 %all_to_all.45 = bf16[2,128,128]{1,2,0:T(8,128)(2,1)S(1)} all-to-all(bf16[2,128,128]{1,2,0:T(8,128)(2,1)S(1)} %broadcast_in_dim.58), channel_id=1, replica_groups=mesh['shard_0'=8,'shard_1'=4,'shard_2'=4,'mp'=2] {'mp'}, dimensions={0} | all-to-all | bytes 131072 | tf_op jit(solution)/shard_map/all_to_all | solution.py:27
  148.6 3.8 all_to_all.46
  152.4 9.2 %all_gather.18 = bf16[512,128]{1,0:T(8,128)(2,1)S(1)} all-gather(bf16[128,128]{1,0:T(8,128)(2,1)S(1)} %add_convert_fusion), channel_id=1, replica_groups=mesh['shard_0'=8,'shard_1'=4,'shard_2'=4,'mp'=2] {'shard_2'}, dimensions={0}, use_global_device_ids=true | all-gather | bytes 163840 | tf_op jit(solution)/shard_map/all_gather | solution.py:21
  161.6 11.1 %all_gather.19 = bf16[2048,128]{1,0:T(8,128)(2,1)} all-gather(bf16[512,128]{1,0:T(8,128)(2,1)S(1)} %all_gather.18), channel_id=1, replica_groups=mesh['shard_0'=8,'shard_1'=4,'shard_2'=4,'mp'=2] {'shard_1'}, dimensions={0}, use_global_device_ids=true | all-gather | bytes 655360 | tf_op jit(solution)/shard_map/all_gather | solution.py:21
  173.4 9.0 %all-to-all-start.4 = ((bf16[2,256,128]{1,2,0:T(8,128)(2,1)}), bf16[2,256,128]{1,2,0:T(8,128)(2,1)S(1)}, u32[]{:S(2)}, u32[]{:S(2)}) async-start(bf16[2,256,128]{1,2,0:T(8,128)(2,1)} %broadcast_in_dim.60), calls=%async_computation.4 | async-start | bytes 262144 | tf_op jit(solution)/shard_map/all_to_all | solution.py:27
  184.9 43.9 %all-gather.3.cloned.1.call-done = bf16[16384,128]{1,0:T(8,128)(2,1)} async-done(((bf16[2048,128]{1,0:T(8,128)(2,1)}), bf16[16384,128]{1,0:T(8,128)(2,1)}) %all-gather.3.cloned.1.call-update) | async-done | bytes 4194320 | tf_op jit(solution)/shard_map/all_gather | solution.py:21
  228.8 2.8 gather_fusion.1
  232.0 1.7 scatter_fusion.1
  233.8 4.3 all_to_all.47
  238.7 2.1 fusion.2
  240.8 1.8 fusion.3
  242.7 4.0 all_to_all.48
  248.2 4.3 broadcast.92
  252.5 3.3 scatter_fusion.2
  255.8 6.3 %convert_element_type.107 = bf16[128,128,128]{2,1,0:T(8,128)(2,1)} convert(f32[128,128,128]{2,1,0:T(8,128)} %scatter_fusion.2) | non-fusion elementwise | flops 2097152 | bytes 12582912 | tf_op jit(solution)/shard_map/convert_element_type | solution.py:78
  262.1 11.8 %all-to-all-start.6 = ((bf16[128,128,128]{2,1,0:T(8,128)(2,1)}), bf16[128,128,128]{2,1,0:T(8,128)(2,1)}, u32[]{:S(2)}, u32[]{:S(2)}) async-start(bf16[128,128,128]{2,1,0:T(8,128)(2,1)} %convert_element_type.107), calls=%async_computation.6 | async-start | bytes 8388608 | tf_op jit(solution)/shard_map/all_to_all | solution.py:77
  274.1 93.5 %all-to-all-done.6 = bf16[128,128,128]{2,1,0:T(8,128)(2,1)} async-done(((bf16[128,128,128]{2,1,0:T(8,128)(2,1)}), bf16[128,128,128]{2,1,0:T(8,128)(2,1)}, u32[]{:S(2)}, u32[]{:S(2)}) %all-to-all-start.6) | async-done | bytes 4194336 | tf_op jit(solution)/shard_map/all_to_all | solution.py:77
  367.6 2.8 reduce_sum.98
  370.5 6.4 %all_to_all.49 = bf16[2,128,128]{1,2,0:T(8,128)(2,1)S(1)} all-to-all(bf16[2,128,128]{1,2,0:T(8,128)(2,1)S(1)} %broadcast_in_dim.62), channel_id=1, replica_groups=mesh['shard_0'=8,'shard_1'=4,'shard_2'=4,'mp'=2] {'mp'}, dimensions={0} | all-to-all | bytes 131072 | tf_op jit(solution)/shard_map/all_to_all | solution.py:27
  377.3 1.6 fusion.34
  380.4 3.8 all_to_all.50
  384.8 9.1 %all_gather.21 = bf16[512,128]{1,0:T(8,128)(2,1)S(1)} all-gather(bf16[128,128]{1,0:T(8,128)(2,1)S(1)} %fusion.42), channel_id=1, replica_groups=mesh['shard_0'=8,'shard_1'=4,'shard_2'=4,'mp'=2] {'shard_2'}, dimensions={0}, use_global_device_ids=true | all-gather | bytes 163840 | tf_op jit(solution)/shard_map/all_gather | solution.py:21
  393.9 10.6 %all_gather.22 = bf16[2048,128]{1,0:T(8,128)(2,1)} all-gather(bf16[512,128]{1,0:T(8,128)(2,1)S(1)} %all_gather.21), channel_id=1, replica_groups=mesh['shard_0'=8,'shard_1'=4,'shard_2'=4,'mp'=2] {'shard_1'}, dimensions={0}, use_global_device_ids=true | all-gather | bytes 655360 | tf_op jit(solution)/shard_map/all_gather | solution.py:21
  404.5 56.6 %all-gather.5.cloned.1.call-done = bf16[16384,128]{1,0:T(8,128)(2,1)} async-done(((bf16[2048,128]{1,0:T(8,128)(2,1)}), bf16[16384,128]{1,0:T(8,128)(2,1)}) %all-gather.5.cloned.1.call-update) | async-done | bytes 4194320 | tf_op jit(solution)/shard_map/all_gather | solution.py:21
  461.2 2.8 gather_fusion.3
  464.4 1.6 scatter_fusion.3
  (106 shorter events, 17.0 us)
Async XLA Ops:
  7.2 231.2 %copy-start = (bf16[256,1024]{1,0:T(8,128)(2,1)S(1)}, bf16[256,1024]{1,0:T(8,128)(2,1)}, u32[]{:S(2)}) copy-start(bf16[256,1024]{1,0:T(8,128)(2,1)} %param.31) | copy-start | bytes 1572868
  7.2 8.8 %copy-start.16 = (s32[16]{0:T(128)S(1)}, s32[16]{0:T(128)}, u32[]{:S(2)}) copy-start(s32[16]{0:T(128)} %param.25) | copy-start | bytes 196
  25.6 120.7 %copy-start.13 = (f32[256]{0:T(256)S(1)}, f32[256]{0:T(256)}, u32[]{:S(2)}) copy-start(f32[256]{0:T(256)} %param.26) | copy-start | bytes 3076
  25.6 120.8 %copy-start.5 = (bf16[256,1024]{1,0:T(8,128)(2,1)S(1)}, bf16[256,1024]{1,0:T(8,128)(2,1)}, u32[]{:S(2)}) copy-start(bf16[256,1024]{1,0:T(8,128)(2,1)} %param.28) | copy-start | bytes 1572868
  25.7 122.6 %copy-start.3 = (bf16[1024,256]{1,0:T(8,128)(2,1)S(1)}, bf16[1024,256]{1,0:T(8,128)(2,1)}, u32[]{:S(2)}) copy-start(bf16[1024,256]{1,0:T(8,128)(2,1)} %param.30) | copy-start | bytes 1572868
  25.7 147.0 %copy-start.9 = (bf16[256,128]{1,0:T(8,128)(2,1)S(1)}, bf16[256,128]{1,0:T(8,128)(2,1)}, u32[]{:S(2)}) copy-start(bf16[256,128]{1,0:T(8,128)(2,1)} %param.22) | copy-start | bytes 196612
  25.7 110.2 %all-to-all-start = ((bf16[128,128,128]{2,1,0:T(8,128)(2,1)}), bf16[128,128,128]{2,1,0:T(8,128)(2,1)}, u32[]{:S(2)}, u32[]{:S(2)}) async-start(bf16[128,128,128]{2,1,0:T(8,128)(2,1)} %convert_element_type.91), calls=%async_computation | async-start | bytes 8388608 | tf_op jit(solution)/shard_map/all_to_all | solution.py:77
  42.7 139.8 %copy-start.12 = (f32[256]{0:T(256)S(1)}, f32[256]{0:T(256)}, u32[]{:S(2)}) copy-start(f32[256]{0:T(256)} %param.27) | copy-start | bytes 3076
  42.7 139.8 %copy-start.17 = (s32[16]{0:T(128)S(1)}, s32[16]{0:T(128)}, u32[]{:S(2)}) copy-start(s32[16]{0:T(128)} %param.25) | copy-start | bytes 196
  42.7 140.9 %copy-start.2 = (bf16[1024,256]{1,0:T(8,128)(2,1)S(1)}, bf16[1024,256]{1,0:T(8,128)(2,1)}, u32[]{:S(2)}) copy-start(bf16[1024,256]{1,0:T(8,128)(2,1)} %param.33) | copy-start | bytes 1572868
  42.7 186.1 %all-gather.3.cloned.1.call-start = ((), (), s32[]{:S(2)}) async-start(), calls=%async_computation.9 | async-start | bytes 4718592 | tf_op jit(solution)/shard_map/all_gather | solution.py:21
  146.3 2.0 copy-start.14
  146.7 5.7 %copy-start.7 = (f32[128,1024]{1,0:T(8,128)}, f32[128,1024]{1,0:T(8,128)S(1)}, u32[]{:S(2)}) copy-start(f32[128,1024]{1,0:T(8,128)S(1)} %fusion.47) | copy-start | bytes 1572868
  148.2 13.3 %copy-start.8 = (f32[128,1024]{1,0:T(8,128)}, f32[128,1024]{1,0:T(8,128)S(1)}, u32[]{:S(2)}) copy-start(f32[128,1024]{1,0:T(8,128)S(1)} %fusion.45) | copy-start | bytes 1572868
  173.4 10.1 %all-to-all-start.4 = ((bf16[2,256,128]{1,2,0:T(8,128)(2,1)}), bf16[2,256,128]{1,2,0:T(8,128)(2,1)S(1)}, u32[]{:S(2)}, u32[]{:S(2)}) async-start(bf16[2,256,128]{1,2,0:T(8,128)(2,1)} %broadcast_in_dim.60), calls=%async_computation.4 | async-start | bytes 262144 | tf_op jit(solution)/shard_map/all_to_all | solution.py:27
  242.6 9.8 %copy-start.18 = (s32[16]{0:T(128)S(1)}, s32[16]{0:T(128)}, u32[]{:S(2)}) copy-start(s32[16]{0:T(128)} %param.25) | copy-start | bytes 196
  262.1 114.8 %copy-start.4 = (bf16[1024,256]{1,0:T(8,128)(2,1)S(1)}, bf16[1024,256]{1,0:T(8,128)(2,1)}, u32[]{:S(2)}) copy-start(bf16[1024,256]{1,0:T(8,128)(2,1)} %param.30) | copy-start | bytes 1572868
  262.1 115.2 %copy-start.6 = (bf16[256,1024]{1,0:T(8,128)(2,1)S(1)}, bf16[256,1024]{1,0:T(8,128)(2,1)}, u32[]{:S(2)}) copy-start(bf16[256,1024]{1,0:T(8,128)(2,1)} %param.28) | copy-start | bytes 1572868
  262.1 105.4 %all-to-all-start.6 = ((bf16[128,128,128]{2,1,0:T(8,128)(2,1)}), bf16[128,128,128]{2,1,0:T(8,128)(2,1)}, u32[]{:S(2)}, u32[]{:S(2)}) async-start(bf16[128,128,128]{2,1,0:T(8,128)(2,1)} %convert_element_type.107), calls=%async_computation.6 | async-start | bytes 8388608 | tf_op jit(solution)/shard_map/all_to_all | solution.py:77
  273.9 110.7 %copy-start.15 = (f32[128]{0:T(128)S(1)}, f32[128]{0:T(128)}, u32[]{:S(2)}) copy-start(f32[128]{0:T(128)} %copy-done.14) | copy-start | bytes 1540
  273.9 110.7 %copy-start.20 = (f32[128]{0:T(128)S(1)}, f32[128]{0:T(128)}, u32[]{:S(2)}) copy-start(f32[128]{0:T(128)} %get-tuple-element.10) | copy-start | bytes 1540
  274.0 187.2 %all-gather.5.cloned.1.call-start = ((), (), s32[]{:S(2)}) async-start(), calls=%async_computation.10 | async-start | bytes 4718592 | tf_op jit(solution)/shard_map/all_gather | solution.py:21
  274.1 190.3 %copy-start.19 = (s32[16]{0:T(128)S(1)}, s32[16]{0:T(128)}, u32[]{:S(2)}) copy-start(s32[16]{0:T(128)} %param.24) | copy-start | bytes 196
  377.0 89.1 %copy-start.1 = (f32[256,128]{1,0:T(8,128)S(1)}, f32[256,128]{1,0:T(8,128)}, u32[]{:S(2)}) copy-start(f32[256,128]{1,0:T(8,128)} %param.19) | copy-start | bytes 393220
  377.0 89.1 %copy-start.10 = (f32[256,128]{1,0:T(8,128)S(1)}, f32[256,128]{1,0:T(8,128)}, u32[]{:S(2)}) copy-start(f32[256,128]{1,0:T(8,128)} %param.20) | copy-start | bytes 393220
  377.0 89.1 %copy-start.11 = (f32[256,128]{1,0:T(8,128)S(1)}, f32[256,128]{1,0:T(8,128)}, u32[]{:S(2)}) copy-start(f32[256,128]{1,0:T(8,128)} %param.21) | copy-start | bytes 393220
Sparse Core Ops, SparseCore 0:
  172.8 55.9 all-gather.2
  404.7 56.4 all-gather.4
where the time goes:
time: 475 us; the launch traced here: 474 us
  waiting for transfers between devices  288 us (61%)
  blocking collectives  69.1 us (15%)
  starting transfers between devices  37.9 us (8%)
  other arithmetic  33.9 us (7%)
  local copies, waits for them, and re-layouts  17.5 us (4%)
  between operations  14.6 us (3%)
  matrix products  12.5 us (3%)
    all_to_all x2, waiting for transfers between devices, owner_sums(): lax.all_to_all(coalesced.astype(jnp.bfloat16), SHARD, split_axis=0, conca...  187 us
    all_gather x2, waiting for transfers between devices, gather_axes(): value = lax.all_gather(value, axis, axis=dim, tiled=True)  101 us
    all_gather x4, blocking collectives, gather_axes(): value = lax.all_gather(value, axis, axis=dim, tiled=True)  39.9 us
    all_to_all x2, starting transfers between devices, owner_sums(): lax.all_to_all(coalesced.astype(jnp.bfloat16), SHARD, split_axis=0, conca...  28.8 us
    all_to_all x5, blocking collectives, sent_to_all(): return lax.all_to_all(copies, axis, split_axis=0, concat_axis=0, tiled=True)  25.3 us
    convert_element_type x2, other arithmetic, owner_sums(): coalesced.astype(jnp.bfloat16)  12.7 us
  transfers between devices with their start and end apart: 5, of which 5 were waited for; matrix products, arithmetic and copies ran while one was open for 0% of the time, Pallas kernels for 0%

commit v1 on v0

v1 whole, which is shorter than its diff:
```python
import jax
import jax.numpy as jnp
from jax import lax
from jax.experimental import pallas as pl
from jax.experimental.pallas import tpu as pltpu
from jax.sharding import PartitionSpec as P

D = 256
HALF = 128
BLOCK = 128
TILE_DEV = 16
RING = 8
PLANE = 16
COLUMNS = 16
OWN = 64
HIDDEN = 1024

NORM_EPSILON = 1e-05
LEARNING_RATE = 0.01
BETA_FIRST = 0.9
BETA_SECOND = 0.99
ADAM_EPSILON = 1e-08

MESH = pl.DeviceIdType.MESH
BF = jnp.bfloat16
F32 = jnp.float32


def dot(a, b):
    return jnp.dot(a, b, preferred_element_type=F32)


def dot_nt(a, b):
    return lax.dot_general(a, b, (((1,), (1,)), ((), ())), preferred_element_type=F32)


def silu_parts(gate_values):
    sigmoid = jax.nn.sigmoid(gate_values)
    return (gate_values * sigmoid, sigmoid * (1.0 + gate_values * (1.0 - sigmoid)))


def rms_scale(values):
    return lax.rsqrt(jnp.mean(values * values, axis=-1, keepdims=True) + NORM_EPSILON)


def rows16(start, size):
    return pl.ds(pl.multiple_of(start, 16), size)


def kernel(
    rows_ref,
    cot_ref,
    bits_ref,
    item_ref,
    dest_ref,
    gain_b_ref,
    gain_i_ref,
    gate_b_ref,
    up_b_ref,
    down_b_ref,
    gate_i_ref,
    up_i_ref,
    down_i_ref,
    back_ref,
    wide,
    tall,
    words_out,
    words_in,
    ring_rows,
    spread_mat,
    collect_mat,
    select_cols,
    select_rows,
    tile_sums,
    owner_out,
    owner_in,
    block_out,
    block_in,
    picked,
    item_out,
    item_in,
    back_in,
    grad_out_buf,
    cot_whole,
    gate_keep,
    up_keep,
    sum_keep,
    weight_own,
    weight_send,
    weight_recv,
    cot_send,
    cot_recv,
    words_send,
    words_recv,
    rows_send,
    rows_recv,
    grad_send,
    grad_recv,
    item_send,
    item_recv,
    back_send,
    back_recv,
    owner_send,
    owner_recv,
    block_send,
    block_recv,
):
    shard = lax.axis_index("shard")
    m = lax.axis_index("mp")
    other = 1 - m
    z = lax.div(shard, PLANE)
    q = lax.rem(shard, PLANE)
    me = 2 * q + m

    def remote(src, dst, send, recv, z_to, q_to, m_to):
        return pltpu.make_async_remote_copy(
            src_ref=src,
            dst_ref=dst,
            send_sem=send,
            recv_sem=recv,
            device_id=(z_to * PLANE + q_to, m_to),
            device_id_type=MESH,
        )

    weights = (
        (gate_b_ref, wide.at[0]),
        (up_b_ref, wide.at[1]),
        (down_b_ref, tall.at[0]),
        (gate_i_ref, wide.at[2]),
        (up_i_ref, wide.at[3]),
        (down_i_ref, tall.at[1]),
    )

    def own_weight(n):
        src, dst = weights[n]
        return pltpu.make_async_copy(src, dst.at[m], weight_own.at[n])

    def sibling_weight(n):
        src, dst = weights[n]
        return remote(src, dst.at[m], weight_send.at[n], weight_recv.at[n], z, q, other)

    barrier = pltpu.get_barrier_semaphore()

    def greet_plane(step, carry):
        k = lax.rem(me + step, 2 * PLANE)
        pl.semaphore_signal(
            barrier,
            inc=1,
            device_id=(z * PLANE + lax.div(k, 2), lax.rem(k, 2)),
            device_id_type=MESH,
        )
        return carry

    def greet_ring(step, carry):
        z_to = lax.rem(z + step, RING)
        for m_to in range(2):
            pl.semaphore_signal(
                barrier, inc=1, device_id=(z_to * PLANE + q, m_to), device_id_type=MESH
            )
        return carry

    lax.fori_loop(1, 2 * PLANE, greet_plane, 0)
    lax.fori_loop(1, RING, greet_ring, 0)
    for n in range(6):
        own_weight(n).start()

    ring_rows[0, z] = rows_ref[...].astype(BF)
    sub = lax.broadcasted_iota(jnp.int32, (8, 128), 0)
    lane = lax.broadcasted_iota(jnp.int32, (8, 128), 1)
    group = lane // COLUMNS
    items = []
    for half in range(2):
        values = jnp.zeros((8, 128), jnp.int32)
        for t in range(8):
            values = jnp.where(group == t, item_ref[half * 8 + t], values)
        items.append(values)
    dests = jnp.zeros((8, 128), jnp.int32)
    for t in range(TILE_DEV):
        dests = jnp.where(lane == z * TILE_DEV + t, dest_ref[t], dests)
    about = jnp.where(sub == 0, items[0], jnp.where(sub == 1, items[1], dests))
    for z_to in range(RING):
        for half in range(2):
            values = jnp.zeros((8, 128), jnp.int32)
            for t in range(8):
                shift = (COLUMNS * (t - z_to)) % 128
                turned = bits_ref[half * 8 + t]
                if shift:
                    turned = pltpu.roll(turned, shift, 1)
                values = jnp.where(group == t, turned, values)
            words_out[z_to, half] = values
        words_out[z_to, 2] = about
    words_in[z] = words_out[z]

    pl.semaphore_wait(barrier, 2 * PLANE - 1 + 2 * (RING - 1))

    def words_copy(z_to):
        return remote(
            words_out.at[z_to], words_in.at[z], words_send.at[z_to], words_recv.at[z], z_to, q, m
        )

    def rows_copy(z_to):
        return remote(
            ring_rows.at[0, z],
            ring_rows.at[0, z],
            rows_send.at[z_to],
            rows_recv.at[z],
            z_to,
            q,
            m,
        )

    def start_ring(step, carry):
        z_to = lax.rem(z + step, RING)
        words_copy(z_to).start()
        rows_copy(z_to).start()
        return carry

    lax.fori_loop(1, RING, start_ring, 0)

    def cot_copy():
        return remote(
            cot_ref.at[rows16(other * BLOCK, BLOCK)],
            cot_whole.at[m],
            cot_send,
            cot_recv,
            z,
            q,
            other,
        )

    for n in range(3):
        sibling_weight(n).start()
    cot_copy().start()
    for n in range(3, 6):
        sibling_weight(n).start()
    cot_whole[m] = cot_ref[rows16(m * BLOCK, BLOCK), :]

    def wait_words(z_from):
        remote(
            words_in.at[z_from],
            words_in.at[z_from],
            words_send.at[z],
            words_recv.at[z_from],
            z,
            q,
            other,
        ).wait_recv()

    def wait_rows(z_from):
        remote(
            ring_rows.at[0, z_from],
            ring_rows.at[0, z_from],
            rows_send.at[z],
            rows_recv.at[z_from],
            z,
            q,
            other,
        ).wait_recv()

    left = lax.broadcasted_iota(jnp.int32, (256, 256), 0)
    right = lax.broadcasted_iota(jnp.int32, (256, 256), 1)
    swap = jnp.where(
        (left // COLUMNS == right % COLUMNS) & (left % COLUMNS == right // COLUMNS), 1.0, 0.0
    ).astype(BF)

    def unpack(z_from):
        about_in = words_in[z_from, 2]
        shifts = lax.broadcasted_iota(jnp.int32, (8, 16, 128), 1)
        halves = []
        for half in range(2):
            packed = jnp.broadcast_to(words_in[z_from, half][:, None, :], (8, 16, 128))
            bits = (jnp.right_shift(packed, shifts) & 1).reshape(128, 128).astype(F32)
            halves.append((bits, jnp.broadcast_to(about_in[half : half + 1, :], (128, 128))))
        blocks = []
        for block in range(2):
            blocks.append(
                jnp.concatenate(
                    [jnp.where(item == block, bits, 0.0) for bits, item in halves], axis=1
                )
            )
        mat = jnp.concatenate(blocks, axis=0).astype(BF)
        spread_mat[z_from] = dot(mat, swap).astype(BF)
        collect_mat[z_from] = dot_nt(swap, mat).astype(BF)

    def add_tiles(phase, z_from):
        sums = dot(collect_mat[z_from], ring_rows[phase, z_from])
        high = sums.astype(BF)
        low = (sums - high.astype(F32)).astype(BF)
        tile_sums[:, rows16(z_from * TILE_DEV, TILE_DEV), :] = high.reshape(16, 16, 128)
        tile_sums[:, rows16(BLOCK + z_from * TILE_DEV, TILE_DEV), :] = low.reshape(16, 16, 128)

    unpack(z)
    add_tiles(0, z)

    def take_ring(step, carry):
        z_from = lax.rem(z + step, RING)
        wait_words(z_from)
        unpack(z_from)
        wait_rows(z_from)
        add_tiles(0, z_from)
        return carry

    lax.fori_loop(1, RING, take_ring, 0)

    all_dest = words_in[0, 2][2:3, :]
    for z_from in range(1, RING):
        all_dest = all_dest + words_in[z_from, 2][2:3, :]
    block_of = lax.broadcasted_iota(jnp.int32, (128, 128), 0)
    column_of = lax.broadcasted_iota(jnp.int32, (128, 128), 1)
    one_hot = jnp.where(block_of == all_dest, 1.0, 0.0).astype(BF)
    select_cols[...] = jnp.concatenate([one_hot, one_hot], axis=1)
    eye = jnp.where(block_of == column_of, 1.0, 0.0).astype(BF)
    select_rows[...] = dot_nt(eye, one_hot).astype(BF)

    def owner_copy(phase, q_to, m_to):
        return remote(
            owner_out.at[phase, q_to, rows16(m_to * OWN, OWN)],
            owner_in.at[phase, q, m],
            owner_send.at[phase, q_to, m_to],
            owner_recv.at[phase, q, m],
            z,
            q_to,
            m_to,
        )

    def block_copy(phase, q_to, m_to):
        return remote(
            block_out.at[phase, m_to],
            block_in.at[phase, q, rows16(m * OWN, OWN)],
            block_send.at[phase, q_to, m_to],
            block_recv.at[phase, q, m],
            z,
            q_to,
            m_to,
        )

    def sum_at_owners(phase):
        def send_column(step, carry):
            j = lax.rem(q + step, PLANE)
            owner_out[phase, j] = dot(select_cols[...], tile_sums[j]).astype(BF)
            for m_to in range(2):
                owner_copy(phase, j, m_to).start()
            return carry

        lax.fori_loop(1, PLANE, send_column, 0)
        owner_out[phase, q] = dot(select_cols[...], tile_sums[q]).astype(BF)
        owner_copy(phase, q, other).start()
        owner_in[phase, q, m] = owner_out[phase, q, rows16(m * OWN, OWN), :]

        def take(step, carry):
            k = lax.rem(me + step, 2 * PLANE)
            q_from, m_from = lax.div(k, 2), lax.rem(k, 2)
            remote(
                owner_in.at[phase, q_from, m_from],
                owner_in.at[phase, q_from, m_from],
                owner_send.at[phase, q, m],
                owner_recv.at[phase, q_from, m_from],
                z,
                q,
                other,
            ).wait_recv()
            return carry

        lax.fori_loop(1, 2 * PLANE, take, 0)
        halves = []
        for m_from in range(2):
            total = owner_in[phase, 0, m_from].astype(F32)
            for q_from in range(1, PLANE):
                total = total + owner_in[phase, q_from, m_from].astype(F32)
            halves.append(total)
        return jnp.concatenate(halves, axis=1)

    def send_blocks(phase, values):
        for m_to in range(2):
            block_out[phase, m_to] = values[:, m_to * HALF : (m_to + 1) * HALF]

        def send(step, carry):
            k = lax.rem(me + step, 2 * PLANE)
            block_copy(phase, lax.div(k, 2), lax.rem(k, 2)).start()
            return carry

        lax.fori_loop(1, 2 * PLANE, send, 0)
        block_in[phase, q, rows16(m * OWN, OWN), :] = block_out[phase, m]

    def wait_block(phase, q_from, m_from):
        remote(
            block_out.at[phase, m_from],
            block_in.at[phase, q_from, rows16(m_from * OWN, OWN)],
            block_send.at[phase, q, m],
            block_recv.at[phase, q_from, m_from],
            z,
            q,
            other,
        ).wait_recv()

    def pick(phase, j):
        chosen = dot(select_rows[...], block_in[phase, j]).astype(BF)
        picked[:, rows16(j * COLUMNS, COLUMNS), :] = chosen.reshape(8, 16, 128)

    def pick_all(phase):
        wait_block(phase, q, other)
        pick(phase, q)

        def step_pick(step, carry):
            j = lax.rem(q + PLANE - step, PLANE)
            for m_from in range(2):
                wait_block(phase, j, m_from)
            pick(phase, j)
            return carry

        lax.fori_loop(1, PLANE, step_pick, 0)

    basket_gain = gain_b_ref[...]
    item_gain = gain_i_ref[...]

    basket_sum = sum_at_owners(0)
    sum_keep[...] = basket_sum
    for n in range(3):
        own_weight(n).wait()
        sibling_weight(n).wait_recv()
    normed = basket_sum * rms_scale(basket_sum) * basket_gain
    normed_bf = normed.astype(BF)
    total = normed
    for h in range(2):
        gate_pre = dot(normed_bf, wide[0, h])
        up_pre = dot(normed_bf, wide[1, h])
        gate_keep[h] = gate_pre
        up_keep[h] = up_pre
        hidden = (gate_pre * jax.nn.sigmoid(gate_pre) * up_pre).astype(BF)
        total = total + dot(hidden, tall[0, h])
    send_blocks(0, total.astype(BF))
    pick_all(0)

    def item_copy(z_to, m_to):
        return remote(
            item_out.at[0, z_to, rows16(m_to * BLOCK, BLOCK)],
            item_in.at[z, m],
            item_send.at[z_to, m_to],
            item_recv.at[z, m],
            z_to,
            q,
            m_to,
        )

    def send_items(step, carry):
        z_to = lax.rem(z + step, RING)
        item_out[0, z_to] = dot(spread_mat[z_to], picked[z_to]).astype(BF)
        for m_to in range(2):
            item_copy(z_to, m_to).start()
        return carry

    lax.fori_loop(1, RING, send_items, 0)
    item_out[0, z] = dot(spread_mat[z], picked[z]).astype(BF)
    item_copy(z, other).start()
    item_in[z, m] = item_out[0, z, rows16(m * BLOCK, BLOCK), :]

    def wait_item(z_from, m_from):
        remote(
            item_in.at[z_from, m_from],
            item_in.at[z_from, m_from],
            item_send.at[z, m],
            item_recv.at[z_from, m_from],
            z,
            q,
            other,
        ).wait_recv()

    for n in range(3, 6):
        own_weight(n).wait()
        sibling_weight(n).wait_recv()
    cot_copy_in = remote(
        cot_whole.at[other], cot_whole.at[other], cot_send, cot_recv, z, q, other
    )
    cot_copy_in.wait_recv()
    wait_item(z, other)

    def take_items(step, carry):
        z_from = lax.rem(z + step, RING)
        for m_from in range(2):
            wait_item(z_from, m_from)
        return carry

    lax.fori_loop(1, RING, take_items, 0)
    halves = []
    for m_from in range(2):
        summed = item_in[0, m_from].astype(F32)
        for z_from in range(1, RING):
            summed = summed + item_in[z_from, m_from].astype(F32)
        halves.append(summed)
    message = jnp.concatenate(halves, axis=1)
    cot_full = jnp.concatenate([cot_whole[0], cot_whole[1]], axis=1)
    scale_item = rms_scale(message)
    query = (message * scale_item * item_gain).astype(BF)
    grad_query = jnp.zeros((BLOCK, D), F32)
    for h in range(2):
        gate_pre = dot(query, wide[2, h])
        up_pre = dot(query, wide[3, h])
        grad_hidden = dot_nt(cot_full, tall[1, h])
        value, slope = silu_parts(gate_pre)
        grad_up = (grad_hidden * value).astype(BF)
        grad_gate = (grad_hidden * up_pre * slope).astype(BF)
        grad_query = grad_query + dot_nt(grad_gate, wide[2, h]) + dot_nt(grad_up, wide[3, h])
    inner = jnp.sum(item_gain * grad_query * message, axis=1, keepdims=True)
    cubed = scale_item * scale_item * scale_item
    grad_message = (scale_item * item_gain * grad_query - message * cubed * inner / D).astype(BF)
    for m_to in range(2):
        grad_out_buf[m_to] = grad_message[:, m_to * HALF : (m_to + 1) * HALF]

    def grad_copy(z_to, m_to):
        return remote(
            grad_out_buf.at[m_to],
            ring_rows.at[1, z, rows16(m * BLOCK, BLOCK)],
            grad_send.at[z_to, m_to],
            grad_recv.at[z, m],
            z_to,
            q,
            m_to,
        )

    def send_grads(step, carry):
        z_to = lax.rem(z + step, RING)
        for m_to in range(2):
            grad_copy(z_to, m_to).start()
        return carry

    grad_copy(z, other).start()
    lax.fori_loop(1, RING, send_grads, 0)
    ring_rows[1, z, rows16(m * BLOCK, BLOCK), :] = grad_out_buf[m]

    def wait_grad(z_from, m_from):
        remote(
            grad_out_buf.at[m_from],
            ring_rows.at[1, z_from, rows16(m_from * BLOCK, BLOCK)],
            grad_send.at[z, m],
            grad_recv.at[z_from, m_from],
            z,
            q,
            other,
        ).wait_recv()

    wait_grad(z, other)
    add_tiles(1, z)

    def take_grads(step, carry):
        z_from = lax.rem(z + step, RING)
        for m_from in range(2):
            wait_grad(z_from, m_from)
        add_tiles(1, z_from)
        return carry

    lax.fori_loop(1, RING, take_grads, 0)
    grad_out = sum_at_owners(1)
    grad_out_bf = grad_out.astype(BF)
    grad_normed = grad_out
    for h in range(2):
        grad_hidden = dot_nt(grad_out_bf, tall[0, h])
        value, slope = silu_parts(gate_keep[h])
        grad_up = (grad_hidden * value).astype(BF)
        grad_gate = (grad_hidden * up_keep[h] * slope).astype(BF)
        grad_normed = grad_normed + (dot_nt(grad_gate, wide[0, h]) + dot_nt(grad_up, wide[1, h]))
    sums = sum_keep[...]
    scale_basket = rms_scale(sums)
    inner_basket = jnp.sum(basket_gain * grad_normed * sums, axis=1, keepdims=True)
    cubed_basket = scale_basket * scale_basket * scale_basket
    grad_sum = scale_basket * basket_gain * grad_normed - sums * cubed_basket * inner_basket / D
    send_blocks(1, grad_sum.astype(BF))
    pick_all(1)

    def back_copy(z_to):
        return remote(
            item_out.at[1, z_to], back_in.at[z], back_send.at[z_to], back_recv.at[z], z_to, q, m
        )

    def send_back(step, carry):
        z_to = lax.rem(z + step, RING)
        item_out[1, z_to] = dot(spread_mat[z_to], picked[z_to]).astype(BF)
        back_copy(z_to).start()
        return carry

    lax.fori_loop(1, RING, send_back, 0)
    back_in[z] = dot(spread_mat[z], picked[z]).astype(BF)

    def take_back(step, carry):
        z_from = lax.rem(z + step, RING)
        remote(
            back_in.at[z_from],
            back_in.at[z_from],
            back_send.at[z],
            back_recv.at[z_from],
            z,
            q,
            other,
        ).wait_recv()
        return carry

    lax.fori_loop(1, RING, take_back, 0)
    back = back_in[0].astype(F32)
    for z_from in range(1, RING):
        back = back + back_in[z_from].astype(F32)
    back_ref[...] = back

    for n in range(6):
        sibling_weight(n).wait_send()
    cot_copy().wait_send()
    item_copy(z, other).wait_send()
    grad_copy(z, other).wait_send()

    def drain_ring(step, carry):
        z_to = lax.rem(z + step, RING)
        words_copy(z_to).wait_send()
        rows_copy(z_to).wait_send()
        for m_to in range(2):
            item_copy(z_to, m_to).wait_send()
            grad_copy(z_to, m_to).wait_send()
        back_copy(z_to).wait_send()
        return carry

    lax.fori_loop(1, RING, drain_ring, 0)

    def drain_plane(step, carry):
        k = lax.rem(me + step, 2 * PLANE)
        q_to, m_to = lax.div(k, 2), lax.rem(k, 2)
        for phase in range(2):
            owner_copy(phase, q_to, m_to).wait_send()
            block_copy(phase, q_to, m_to).wait_send()
        return carry

    lax.fori_loop(1, 2 * PLANE, drain_plane, 0)


def local(
    item_rows,
    first_moment,
    second_moment,
    item_cot,
    tile_bits,
    tile_item,
    tile_dest,
    basket_gain,
    item_gain,
    gate_basket,
    up_basket,
    down_basket,
    gate_item,
    up_item,
    down_item,
):
    vmem = pl.BlockSpec(memory_space=pltpu.VMEM)
    smem = pl.BlockSpec(memory_space=pltpu.SMEM)
    anywhere = pl.BlockSpec(memory_space=pl.ANY)
    dma = pltpu.SemaphoreType.DMA
    back_items = pl.pallas_call(
        kernel,
        out_shape=jax.ShapeDtypeStruct((2 * BLOCK, HALF), F32),
        in_specs=[vmem, vmem, vmem, smem, smem, vmem, vmem] + [anywhere] * 6,
        out_specs=vmem,
        scratch_shapes=[
            pltpu.VMEM((4, 2, D, HIDDEN), BF),
            pltpu.VMEM((2, 2, HIDDEN, D), BF),
            pltpu.VMEM((RING, 3, 8, 128), jnp.int32),
            pltpu.VMEM((RING, 3, 8, 128), jnp.int32),
            pltpu.VMEM((2, RING, 2 * BLOCK, HALF), BF),
            pltpu.VMEM((RING, 256, 256), BF),
            pltpu.VMEM((RING, 256, 256), BF),
            pltpu.VMEM((128, 256), BF),
            pltpu.VMEM((128, 128), BF),
            pltpu.VMEM((COLUMNS, 256, HALF), BF),
            pltpu.VMEM((2, PLANE, 128, HALF), BF),
            pltpu.VMEM((2, PLANE, 2, OWN, HALF), BF),
            pltpu.VMEM((2, 2, OWN, HALF), BF),
            pltpu.VMEM((2, PLANE, 128, HALF), BF),
            pltpu.VMEM((RING, 256, HALF), BF),
            pltpu.VMEM((2, RING, 256, HALF), BF),
            pltpu.VMEM((RING, 2, BLOCK, HALF), BF),
            pltpu.VMEM((RING, 256, HALF), BF),
            pltpu.VMEM((2, BLOCK, HALF), BF),
            pltpu.VMEM((2, BLOCK, HALF), BF),
            pltpu.VMEM((2, OWN, HIDDEN), F32),
            pltpu.VMEM((2, OWN, HIDDEN), F32),
            pltpu.VMEM((OWN, D), F32),
            dma((6,)),
            dma((6,)),
            dma((6,)),
            dma,
            dma,
            dma((RING,)),
            dma((RING,)),
            dma((RING,)),
            dma((RING,)),
            dma((RING, 2)),
            dma((RING, 2)),
            dma((RING, 2)),
            dma((RING, 2)),
            dma((RING,)),
            dma((RING,)),
            dma((2, PLANE, 2)),
            dma((2, PLANE, 2)),
            dma((2, PLANE, 2)),
            dma((2, PLANE, 2)),
        ],
        compiler_params=pltpu.CompilerParams(
            collective_id=0, has_side_effects=True, vmem_limit_bytes=48 * 1024 * 1024
        ),
        name="layer",
    )(
        item_rows,
        item_cot,
        tile_bits,
        tile_item,
        tile_dest,
        basket_gain.reshape(1, D),
        item_gain.reshape(1, D),
        gate_basket,
        up_basket,
        down_basket,
        gate_item,
        up_item,
        down_item,
    )
    gradient = item_cot.astype(F32) + back_items
    new_first = BETA_FIRST * first_moment + (1.0 - BETA_FIRST) * gradient
    new_second = BETA_SECOND * second_moment + (1.0 - BETA_SECOND) * gradient * gradient
    new_rows = item_rows - LEARNING_RATE * new_first / (jnp.sqrt(new_second) + ADAM_EPSILON)
    return (new_rows, new_first, new_second)


def solution(mesh):
    split = P("shard", "mp")
    return jax.shard_map(
        local,
        mesh=mesh,
        in_specs=(
            split,
            split,
            split,
            split,
            P("shard", None, None),
            P("shard"),
            P("shard"),
            P(),
            P(),
            P(None, "mp"),
            P(None, "mp"),
            P("mp", None),
            P(None, "mp"),
            P(None, "mp"),
            P("mp", None),
        ),
        out_specs=(split, split, split),
        check_vma=False,
    )
```

time: 475 us -> 133 us (0.28)
  waiting for transfers between devices: 288 us -> 0 us
  Pallas kernels: 0 us -> 122 us
  blocking collectives: 69.1 us -> 0 us
  starting transfers between devices: 37.9 us -> 0 us
  other arithmetic: 33.9 us -> 0.79 us
  between operations: 14.6 us -> 0.7 us
  matrix products: 12.5 us -> 0 us
  local copies, waits for them, and re-layouts: 17.5 us -> 9.52 us
    all_to_all x3 -> x0, waiting for transfers between devices: 188 us -> none  [the longest x2 187 us: owner_sums(): lax.all_to_all(coalesced.astype(jnp.bfloat16), SHARD, split_axis=0, conca...]
    pallas_call x0 -> x1, Pallas kernels: none -> 122 us  [local(): pl.pallas_call(kernel, out_shape=jax.ShapeDtypeStruct((2 * BLOCK, HALF),...]
    all_gather x2 -> x0, waiting for transfers between devices: 101 us -> none  [gather_axes(): value = lax.all_gather(value, axis, axis=dim, tiled=True)]
    all_gather x4 -> x0, blocking collectives: 39.9 us -> none  [gather_axes(): value = lax.all_gather(value, axis, axis=dim, tiled=True)]
    all_to_all x3 -> x0, starting transfers between devices: 37.8 us -> none  [the longest x2 28.8 us: owner_sums(): lax.all_to_all(coalesced.astype(jnp.bfloat16), SHARD, split_axis=0, conca...]
    all_to_all x6 -> x0, blocking collectives: 29.1 us -> none  [the longest x5 25.3 us: sent_to_all(): return lax.all_to_all(copies, axis, split_axis=0, concat_axis=0, tiled=True)]
    convert_element_type x9 -> x0, other arithmetic: 15.1 us -> none  [the longest x2 12.7 us: owner_sums(): coalesced.astype(jnp.bfloat16)]
    dot_general x14 -> x0, matrix products: 12.5 us -> none  [the longest x1 2.13 us: local(): jnp.einsum('rh,dh->rd', grad_gate, gate_item, preferred_element_type=jnp....]
  transfers between devices with their start and end apart: 5 -> 0, of which waited for: 5 -> 0; matrix products, arithmetic and copies ran while one was open for 0% -> 0% of each run, Pallas kernels for 0% -> 0%
where the time goes in v1:
time: 133 us
  Pallas kernels  122 us (92%)
  local copies, waits for them, and re-layouts  9.52 us (7%)
    pallas_call x1, Pallas kernels, local(): pl.pallas_call(kernel, out_shape=jax.ShapeDtypeStruct((2 * BLOCK, HALF),...  122 us
    unnamed x30, local copies, waits for them, and re-layouts  9.52 us

profile of v1, /device:TPU:1, one launch (start us, length us, event | category | flops | bytes accessed | tf_op | source)
XLA Modules:
  0.0 132.8 jit_solution(2417562415536510833)
XLA Ops:
  0.6 0.0 copy-start.10
  0.6 0.0 copy-start.12
  0.7 0.0 copy-start.9
  0.7 0.0 copy-start.11
  0.7 0.6 copy-done.10
  1.3 0.0 copy-done.12
  1.3 0.0 copy-done.9
  1.3 0.0 copy-done.11
  1.4 0.0 copy-start
  1.4 0.9 copy-done
  2.3 0.0 copy-start.1
  2.3 1.0 copy-done.1
  3.3 0.0 copy-start.2
  3.3 1.0 copy-done.2
  4.3 0.0 copy-start.3
  4.3 1.0 copy-done.3
  5.4 0.0 copy-start.4
  5.4 1.0 copy-done.4
  6.4 0.0 copy-start.5
  6.4 1.0 copy-done.5
  7.5 0.0 copy-start.6
  7.5 1.0 copy-done.6
  8.5 0.0 copy-start.7
  8.5 0.8 copy-done.7
  9.3 0.0 copy-start.8
  9.4 0.8 copy-done.8
  10.2 0.0 copy-start.13
  10.2 0.0 copy-start.14
  10.2 121.8 %layer.1 = f32[256,128]{1,0:T(8,128)S(1)} custom-call(f32[256,128]{1,0:T(8,128)S(1)} %copy-done, bf16[256,128]{1,0:T(8,128)(2,1)S(1)} %copy-done.7, s32[16,8,128]{2,1,0:T(8,128)S(1)} %copy-done.8, s32[16]{0:T(128)S(1)} %copy-done.11, s32[16]{0:T(128)S(1)} %copy-done.12, f32[1,256]{1,0:T(1,128)S(1)} %bitcast.2, f32[1,256]{1,0:T(1,128)S(1)} %bitcast.3, ...), custom_call_target="tpu_custom_call" | custom-call | tf_op jit(solution)/shard_map/layer/pallas_call | solution.py:652
  132.0 0.0 copy-done.13
  132.0 0.0 copy-done.14
  132.0 0.8 divide_subtract_fusion
Async XLA Ops:
  0.6 0.7 copy-start.10
  0.6 0.7 copy-start.12
  0.7 0.7 copy-start.9
  0.7 0.7 copy-start.11
  1.4 0.9 copy-start
  2.3 1.0 copy-start.1
  3.3 1.0 copy-start.2
  4.3 1.0 copy-start.3
  5.4 1.0 copy-start.4
  6.4 1.0 copy-start.5
  7.5 1.0 copy-start.6
  8.5 0.8 copy-start.7
  9.3 0.8 copy-start.8
  10.2 121.8 %copy-start.13 = (f32[256,128]{1,0:T(8,128)S(1)}, f32[256,128]{1,0:T(8,128)}, u32[]{:S(2)}) copy-start(f32[256,128]{1,0:T(8,128)} %param.16) | copy-start | bytes 393220
  10.2 121.8 %copy-start.14 = (f32[256,128]{1,0:T(8,128)S(1)}, f32[256,128]{1,0:T(8,128)}, u32[]{:S(2)}) copy-start(f32[256,128]{1,0:T(8,128)} %param.17) | copy-start | bytes 393220

commit v2 on v0

v2 whole, which is shorter than its diff:
```python
import jax
import jax.numpy as jnp
from jax import lax
from jax.experimental import pallas as pl
from jax.experimental.pallas import tpu as pltpu
from jax.sharding import PartitionSpec as P

D = 256
HALF = 128
BLOCK = 128
TILE_DEV = 16
RING = 8
PLANE = 16
OWN = 64
HIDDEN = 1024

NORM_EPSILON = 1e-05
LEARNING_RATE = 0.01
BETA_FIRST = 0.9
BETA_SECOND = 0.99
ADAM_EPSILON = 1e-08

MESH = pl.DeviceIdType.MESH
BF = jnp.bfloat16
F32 = jnp.float32


def dot(a, b):
    return jnp.dot(a, b, preferred_element_type=F32)


def dot_nt(a, b):
    return lax.dot_general(a, b, (((1,), (1,)), ((), ())), preferred_element_type=F32)


def silu_parts(gate_values):
    sigmoid = jax.nn.sigmoid(gate_values)
    return (gate_values * sigmoid, sigmoid * (1.0 + gate_values * (1.0 - sigmoid)))


def rms_scale(values):
    return lax.rsqrt(jnp.mean(values * values, axis=-1, keepdims=True) + NORM_EPSILON)


def rows16(start, size):
    return pl.ds(pl.multiple_of(start, 16), size)


def mode_scratch(members, columns):
    dma = pltpu.SemaphoreType.DMA
    wide = TILE_DEV * columns
    tiles = TILE_DEV * members
    slots = wide // 128 + 1
    return {
        "words_out": pltpu.VMEM((members, slots, 8, 128), jnp.int32),
        "words_in": pltpu.VMEM((members, slots, 8, 128), jnp.int32),
        "rows": pltpu.VMEM((2, members, 2 * BLOCK, HALF), BF),
        "spread": pltpu.VMEM((members, 2 * BLOCK, wide), BF),
        "collect": pltpu.VMEM((members, wide, 2 * BLOCK), BF),
        "select_cols": pltpu.VMEM((BLOCK, 2 * tiles), BF),
        "select_rows": pltpu.VMEM((tiles, BLOCK), BF),
        "tile_sums": pltpu.VMEM((columns, 2 * tiles, HALF), BF),
        "owner_out": pltpu.VMEM((2, columns, BLOCK, HALF), BF),
        "owner_in": pltpu.VMEM((2, columns, OWN, HALF), BF),
        "block_out": pltpu.VMEM((2, OWN, HALF), BF),
        "block_in": pltpu.VMEM((2, columns, BLOCK, HALF), BF),
        "picked": pltpu.VMEM((members, wide, HALF), BF),
        "item_out": pltpu.VMEM((2, members, 2 * BLOCK, HALF), BF),
        "item_in": pltpu.VMEM((members, BLOCK, HALF), BF),
        "back_in": pltpu.VMEM((members, 2 * BLOCK, HALF), BF),
        "grad_out": pltpu.VMEM((BLOCK, HALF), BF),
        "words_send": dma((members,)),
        "words_recv": dma((members,)),
        "rows_send": dma((members,)),
        "rows_recv": dma((members,)),
        "owner_send": dma((2, columns, 2)),
        "owner_recv": dma((2, columns)),
        "block_send": dma((2, columns)),
        "block_recv": dma((2, columns, 2)),
        "item_send": dma((members, 2)),
        "item_recv": dma((members,)),
        "grad_send": dma((members,)),
        "grad_recv": dma((members, 2)),
        "back_send": dma((members,)),
        "back_recv": dma((members,)),
    }


def common_scratch():
    dma = pltpu.SemaphoreType.DMA
    return {
        "wide": pltpu.VMEM((4, 2, D, HIDDEN), BF),
        "tall": pltpu.VMEM((2, 2, HIDDEN, D), BF),
        "cot_whole": pltpu.VMEM((2, BLOCK, HALF), BF),
        "gate_keep": pltpu.VMEM((2, OWN, HIDDEN), F32),
        "up_keep": pltpu.VMEM((2, OWN, HIDDEN), F32),
        "sum_keep": pltpu.VMEM((OWN, D), F32),
        "item_rows": pltpu.VMEM((2 * BLOCK, HALF), F32),
        "tile_bits": pltpu.VMEM((TILE_DEV, 8, 128), jnp.int32),
        "load_sem": dma((3,)),
        "weight_own": dma((6,)),
        "weight_send": dma((6,)),
        "weight_recv": dma((6,)),
        "cot_send": dma,
        "cot_recv": dma,
    }


class Mode:
    def __init__(self, core, refs, z, q):
        self.core = core
        self.members, self.columns = (RING, PLANE) if core == 0 else (PLANE, RING)
        self.own_member, self.own_column = (z, q) if core == 0 else (q, z)
        self.z, self.q = z, q
        self.__dict__.update(refs)

    def item_shard(self, member):
        return member * PLANE + self.q if self.core == 0 else self.z * PLANE + member

    def basket_shard(self, column):
        return self.z * PLANE + column if self.core == 0 else column * PLANE + self.q


def kernel(
    rows_hbm,
    cot_hbm,
    bits_hbm,
    item_ref,
    dest_ref,
    gain_b_ref,
    gain_i_ref,
    gate_b_ref,
    up_b_ref,
    down_b_ref,
    gate_i_ref,
    up_i_ref,
    down_i_ref,
    back_ref,
    common,
    ring_refs,
    plane_refs,
):
    shard = lax.axis_index("shard")
    m = lax.axis_index("mp")
    other = 1 - m
    z = lax.div(shard, PLANE)
    q = lax.rem(shard, PLANE)
    me = 2 * q + m
    modes = (Mode(0, ring_refs, z, q), Mode(1, plane_refs, z, q))
    wide, tall, cot_whole = common["wide"], common["tall"], common["cot_whole"]
    gate_keep, up_keep, sum_keep = common["gate_keep"], common["up_keep"], common["sum_keep"]
    rows_ref, bits_ref, load_sem = common["item_rows"], common["tile_bits"], common["load_sem"]
    weight_own, weight_send = common["weight_own"], common["weight_send"]
    weight_recv = common["weight_recv"]
    cot_send, cot_recv = common["cot_send"], common["cot_recv"]

    def remote(src, dst, send, recv, to_shard, to_core):
        return pltpu.make_async_remote_copy(
            src_ref=src,
            dst_ref=dst,
            send_sem=send,
            recv_sem=recv,
            device_id=(to_shard, to_core),
            device_id_type=MESH,
        )

    def arrival(dst, send, recv):
        return remote(dst, dst, send, recv, shard, other)

    def around(count, own, body):
        def step(n, carry):
            body(lax.rem(own + n, count))
            return carry

        lax.fori_loop(1, count, step, 0)

    def back_around(count, own, body):
        def step(n, carry):
            body(lax.rem(own + count - n, count))
            return carry

        lax.fori_loop(1, count, step, 0)

    def per_mode(body):
        for mode in modes:

            @pl.when(m == mode.core)
            def _(mode=mode):
                body(mode)

    weights = (
        (gate_b_ref, wide.at[0]),
        (up_b_ref, wide.at[1]),
        (down_b_ref, tall.at[0]),
        (gate_i_ref, wide.at[2]),
        (up_i_ref, wide.at[3]),
        (down_i_ref, tall.at[1]),
    )

    def own_weight(n):
        src, dst = weights[n]
        return pltpu.make_async_copy(src, dst.at[m], weight_own.at[n])

    def sibling_weight(n):
        src, dst = weights[n]
        return remote(src, dst.at[m], weight_send.at[n], weight_recv.at[n], shard, other)

    load_rows = pltpu.make_async_copy(rows_hbm, rows_ref, load_sem.at[0])
    load_bits = pltpu.make_async_copy(bits_hbm, bits_ref, load_sem.at[1])
    load_cot = pltpu.make_async_copy(
        cot_hbm.at[rows16(m * BLOCK, BLOCK)], cot_whole.at[m], load_sem.at[2]
    )
    load_rows.start()
    load_bits.start()

    barrier = pltpu.get_barrier_semaphore()

    def greet(to_shard, to_core):
        pl.semaphore_signal(
            barrier, inc=1, device_id=(to_shard, to_core), device_id_type=MESH
        )

    def greet_ring(z_to):
        for core in range(2):
            greet(z_to * PLANE + q, core)

    around(RING, z, greet_ring)
    around(2 * PLANE, me, lambda k: greet(z * PLANE + lax.div(k, 2), lax.rem(k, 2)))
    load_cot.start()
    for n in range(6):
        own_weight(n).start()

    sub = lax.broadcasted_iota(jnp.int32, (8, 128), 0)
    lane = lax.broadcasted_iota(jnp.int32, (8, 128), 1)

    def prepare(mode):
        mode.rows[0, mode.own_member] = rows_ref[...].astype(BF)
        columns = mode.columns
        per_slot = 128 // columns
        slots = TILE_DEV // per_slot
        if mode.core == 0:
            tiles = [bits_ref[t] for t in range(TILE_DEV)]
        else:
            left = lax.broadcasted_iota(jnp.int32, (128, 128), 0)
            right = lax.broadcasted_iota(jnp.int32, (128, 128), 1)
            order = jnp.where(
                (left % PLANE == right // columns) & (left // PLANE == right % columns), 1.0, 0.0
            ).astype(BF)
            words = bits_ref[...].reshape(128, 128)
            low = dot((words & 255).astype(F32).astype(BF), order)
            high = dot(jnp.right_shift(words, 8).astype(F32).astype(BF), order)
            words = (low + 256.0 * high).astype(jnp.int32).reshape(TILE_DEV, 8, 128)
            tiles = [words[t] for t in range(TILE_DEV)]
        group = lane // columns
        about = jnp.zeros((8, 128), jnp.int32)
        start = mode.own_member * TILE_DEV
        dest_sub = 2 + lax.div(start, 128)
        dest_lane = lax.rem(start, 128)
        for t in range(TILE_DEV):
            slot, place = t // per_slot, t % per_slot
            about = jnp.where((sub == slot) & (group == place), item_ref[t], about)
            about = jnp.where((sub == dest_sub) & (lane == dest_lane + t), dest_ref[t], about)
        for member in range(mode.members):
            for slot in range(slots):
                values = jnp.zeros((8, 128), jnp.int32)
                for place in range(per_slot):
                    turned = tiles[slot * per_slot + place]
                    shift = (columns * (place - member)) % 128
                    if shift:
                        turned = pltpu.roll(turned, shift, 1)
                    values = jnp.where(group == place, turned, values)
                mode.words_out[member, slot] = values
            mode.words_out[member, slots] = about
        mode.words_in[mode.own_member] = mode.words_out[mode.own_member]

    load_rows.wait()
    load_bits.wait()
    per_mode(prepare)

    pl.semaphore_wait(barrier, 2 * PLANE - 1 + 2 * (RING - 1))

    def words_copy(mode, member):
        return remote(
            mode.words_out.at[member],
            mode.words_in.at[mode.own_member],
            mode.words_send.at[member],
            mode.words_recv.at[mode.own_member],
            mode.item_shard(member),
            mode.core,
        )

    def rows_copy(mode, member):
        return remote(
            mode.rows.at[0, mode.own_member],
            mode.rows.at[0, mode.own_member],
            mode.rows_send.at[member],
            mode.rows_recv.at[mode.own_member],
            mode.item_shard(member),
            mode.core,
        )

    def start_rows(mode):
        around(mode.members, mode.own_member, lambda member: words_copy(mode, member).start())
        around(mode.members, mode.own_member, lambda member: rows_copy(mode, member).start())

    per_mode(start_rows)

    def cot_copy():
        return remote(
            cot_hbm.at[rows16(other * BLOCK, BLOCK)],
            cot_whole.at[m],
            cot_send,
            cot_recv,
            shard,
            other,
        )

    for n in range(3):
        sibling_weight(n).start()
    cot_copy().start()
    for n in range(3, 6):
        sibling_weight(n).start()

    def add_tiles(mode, phase, member):
        sums = dot(mode.collect[member], mode.rows[phase, member])
        high = sums.astype(BF)
        low = (sums - high.astype(F32)).astype(BF)
        shape = (mode.columns, TILE_DEV, HALF)
        tiles = TILE_DEV * mode.members
        mode.tile_sums[:, rows16(member * TILE_DEV, TILE_DEV), :] = high.reshape(shape)
        mode.tile_sums[:, rows16(tiles + member * TILE_DEV, TILE_DEV), :] = low.reshape(shape)

    def take_rows(mode):
        size = TILE_DEV * mode.columns
        slots = size // 128
        left = lax.broadcasted_iota(jnp.int32, (size, size), 0)
        right = lax.broadcasted_iota(jnp.int32, (size, size), 1)

        def turn(tile_major, column_major):
            same = (tile_major // mode.columns == column_major % TILE_DEV) & (
                tile_major % mode.columns == column_major // TILE_DEV
            )
            return jnp.where(same, 1.0, 0.0).astype(BF)

        to_columns = turn(left, right)
        from_tiles = turn(right, left)
        shifts = lax.broadcasted_iota(jnp.int32, (8, 16, 128), 1)

        def unpack(member):
            about = mode.words_in[member, slots]
            halves = []
            for slot in range(slots):
                packed = jnp.broadcast_to(mode.words_in[member, slot][:, None, :], (8, 16, 128))
                bits = (jnp.right_shift(packed, shifts) & 1).reshape(128, 128).astype(F32)
                halves.append((bits, jnp.broadcast_to(about[slot : slot + 1, :], (128, 128))))
            blocks = []
            for block in range(2):
                parts = [jnp.where(item == block, bits, 0.0) for bits, item in halves]
                blocks.append(parts[0] if slots == 1 else jnp.concatenate(parts, axis=1))
            mat = jnp.concatenate(blocks, axis=0).astype(BF)
            mode.spread[member] = dot(mat, to_columns).astype(BF)
            mode.collect[member] = dot_nt(from_tiles, mat).astype(BF)

        def take_words(member):
            arrival(
                mode.words_in.at[member],
                mode.words_send.at[member],
                mode.words_recv.at[member],
            ).wait_recv()
            unpack(member)

        unpack(mode.own_member)
        back_around(mode.members, mode.own_member, take_words)

        tiles = TILE_DEV * mode.members
        about = mode.words_in[0, slots]
        for member in range(1, mode.members):
            about = about + mode.words_in[member, slots]
        all_dest = about[2:3, :]
        if tiles > 128:
            all_dest = jnp.concatenate([all_dest, about[3:4, :]], axis=1)
        block_of = lax.broadcasted_iota(jnp.int32, (BLOCK, tiles), 0)
        one_hot = jnp.where(block_of == all_dest, 1.0, 0.0).astype(BF)
        mode.select_cols[...] = jnp.concatenate([one_hot, one_hot], axis=1)
        eye_left = lax.broadcasted_iota(jnp.int32, (tiles, tiles), 0)
        eye_right = lax.broadcasted_iota(jnp.int32, (tiles, tiles), 1)
        eye = jnp.where(eye_left == eye_right, 1.0, 0.0).astype(BF)
        mode.select_rows[...] = lax.dot_general(
            eye, one_hot, (((1,), (1,)), ((), ())), preferred_element_type=F32
        ).astype(BF)

        add_tiles(mode, 0, mode.own_member)

        def take(member):
            arrival(
                mode.rows.at[0, member], mode.rows_send.at[member], mode.rows_recv.at[member]
            ).wait_recv()
            add_tiles(mode, 0, member)

        back_around(mode.members, mode.own_member, take)

    per_mode(take_rows)

    def owner_copy(mode, phase, column, to_core):
        return remote(
            mode.owner_out.at[phase, column, rows16(to_core * OWN, OWN)],
            mode.owner_in.at[phase, mode.own_column],
            mode.owner_send.at[phase, column, to_core],
            mode.owner_recv.at[phase, mode.own_column],
            mode.basket_shard(column),
            to_core,
        )

    def send_sums(mode, phase):
        def column_sum(column):
            mode.owner_out[phase, column] = dot(
                mode.select_cols[...], mode.tile_sums[column]
            ).astype(BF)

        def send(column):
            column_sum(column)
            for to_core in range(2):
                owner_copy(mode, phase, column, to_core).start()

        around(mode.columns, mode.own_column, send)
        column_sum(mode.own_column)
        owner_copy(mode, phase, mode.own_column, 1 - mode.core).start()
        mode.owner_in[phase, mode.own_column] = mode.owner_out[
            phase, mode.own_column, mode.core * OWN : (mode.core + 1) * OWN, :
        ]

    def sum_at_owners(phase):
        per_mode(lambda mode: send_sums(mode, phase))
        for mode in modes:

            def take(column, mode=mode):
                arrival(
                    mode.owner_in.at[phase, column],
                    mode.owner_send.at[phase, column, 0],
                    mode.owner_recv.at[phase, column],
                ).wait_recv()

            back_around(mode.columns, mode.own_column, take)

            @pl.when(m != mode.core)
            def _(mode=mode, take=take):
                take(mode.own_column)

        halves = []
        for mode in modes:
            total = mode.owner_in[phase, 0].astype(F32)
            for column in range(1, mode.columns):
                total = total + mode.owner_in[phase, column].astype(F32)
            halves.append(total)
        return jnp.concatenate(halves, axis=1)

    def block_copy(mode, phase, column):
        return remote(
            mode.block_out.at[phase],
            mode.block_in.at[phase, mode.own_column, rows16(m * OWN, OWN)],
            mode.block_send.at[phase, column],
            mode.block_recv.at[phase, mode.own_column, m],
            mode.basket_shard(column),
            mode.core,
        )

    def send_blocks(phase, values):
        for mode in modes:
            mode.block_out[phase] = values[:, mode.core * HALF : (mode.core + 1) * HALF]
        for mode in modes:

            @pl.when(m != mode.core)
            def _(mode=mode):
                block_copy(mode, phase, mode.own_column).start()

            around(
                mode.columns,
                mode.own_column,
                lambda column, mode=mode: block_copy(mode, phase, column).start(),
            )

            @pl.when(m == mode.core)
            def _(mode=mode):
                place = slice(mode.core * OWN, (mode.core + 1) * OWN)
                mode.block_in[phase, mode.own_column, place, :] = mode.block_out[phase]

    def wait_block(mode, phase, column, from_core):
        arrival(
            mode.block_in.at[phase, column, rows16(from_core * OWN, OWN)],
            mode.block_send.at[phase, column],
            mode.block_recv.at[phase, column, from_core],
        ).wait_recv()

    def pick_all(mode, phase):
        def pick(column):
            chosen = dot(mode.select_rows[...], mode.block_in[phase, column]).astype(BF)
            mode.picked[:, rows16(column * TILE_DEV, TILE_DEV), :] = chosen.reshape(
                mode.members, TILE_DEV, HALF
            )

        def take(column):
            for from_core in range(2):
                wait_block(mode, phase, column, from_core)
            pick(column)

        wait_block(mode, phase, mode.own_column, 1 - mode.core)
        pick(mode.own_column)
        back_around(mode.columns, mode.own_column, take)

    basket_gain = gain_b_ref[...]
    item_gain = gain_i_ref[...]

    basket_sum = sum_at_owners(0)
    sum_keep[...] = basket_sum
    for n in range(3):
        own_weight(n).wait()
        sibling_weight(n).wait_recv()
    normed = basket_sum * rms_scale(basket_sum) * basket_gain
    normed_bf = normed.astype(BF)
    total = normed
    for h in range(2):
        gate_pre = dot(normed_bf, wide[0, h])
        up_pre = dot(normed_bf, wide[1, h])
        gate_keep[h] = gate_pre
        up_keep[h] = up_pre
        hidden = (gate_pre * jax.nn.sigmoid(gate_pre) * up_pre).astype(BF)
        total = total + dot(hidden, tall[0, h])
    send_blocks(0, total.astype(BF))

    def item_copy(mode, member, to_core):
        return remote(
            mode.item_out.at[0, member, rows16(to_core * BLOCK, BLOCK)],
            mode.item_in.at[mode.own_member],
            mode.item_send.at[member, to_core],
            mode.item_recv.at[mode.own_member],
            mode.item_shard(member),
            to_core,
        )

    def send_items(mode):
        pick_all(mode, 0)

        def partial(member):
            mode.item_out[0, member] = dot(mode.spread[member], mode.picked[member]).astype(BF)

        def send(member):
            partial(member)
            for to_core in range(2):
                item_copy(mode, member, to_core).start()

        around(mode.members, mode.own_member, send)
        partial(mode.own_member)
        item_copy(mode, mode.own_member, 1 - mode.core).start()
        mode.item_in[mode.own_member] = mode.item_out[
            0, mode.own_member, mode.core * BLOCK : (mode.core + 1) * BLOCK, :
        ]

    per_mode(send_items)

    for n in range(3, 6):
        own_weight(n).wait()
        sibling_weight(n).wait_recv()
    arrival(cot_whole.at[other], cot_send, cot_recv).wait_recv()
    load_cot.wait()
    for mode in modes:

        def take_item(member, mode=mode):
            arrival(
                mode.item_in.at[member], mode.item_send.at[member, 0], mode.item_recv.at[member]
            ).wait_recv()

        back_around(mode.members, mode.own_member, take_item)

        @pl.when(m != mode.core)
        def _(mode=mode, take_item=take_item):
            take_item(mode.own_member)

    halves = []
    for mode in modes:
        summed = mode.item_in[0].astype(F32)
        for member in range(1, mode.members):
            summed = summed + mode.item_in[member].astype(F32)
        halves.append(summed)
    message = jnp.concatenate(halves, axis=1)
    cot_full = jnp.concatenate([cot_whole[0], cot_whole[1]], axis=1)
    scale_item = rms_scale(message)
    query = (message * scale_item * item_gain).astype(BF)
    grad_query = jnp.zeros((BLOCK, D), F32)
    for h in range(2):
        gate_pre = dot(query, wide[2, h])
        up_pre = dot(query, wide[3, h])
        grad_hidden = dot_nt(cot_full, tall[1, h])
        value, slope = silu_parts(gate_pre)
        grad_up = (grad_hidden * value).astype(BF)
        grad_gate = (grad_hidden * up_pre * slope).astype(BF)
        grad_query = grad_query + dot_nt(grad_gate, wide[2, h]) + dot_nt(grad_up, wide[3, h])
    inner = jnp.sum(item_gain * grad_query * message, axis=1, keepdims=True)
    cubed = scale_item * scale_item * scale_item
    grad_message = (scale_item * item_gain * grad_query - message * cubed * inner / D).astype(BF)

    def grad_copy(mode, member):
        return remote(
            mode.grad_out,
            mode.rows.at[1, mode.own_member, rows16(m * BLOCK, BLOCK)],
            mode.grad_send.at[member],
            mode.grad_recv.at[mode.own_member, m],
            mode.item_shard(member),
            mode.core,
        )

    for mode in modes:
        mode.grad_out[...] = grad_message[:, mode.core * HALF : (mode.core + 1) * HALF]
    for mode in modes:

        @pl.when(m != mode.core)
        def _(mode=mode):
            grad_copy(mode, mode.own_member).start()

        around(
            mode.members,
            mode.own_member,
            lambda member, mode=mode: grad_copy(mode, member).start(),
        )

        @pl.when(m == mode.core)
        def _(mode=mode):
            place = slice(mode.core * BLOCK, (mode.core + 1) * BLOCK)
            mode.rows[1, mode.own_member, place, :] = mode.grad_out[...]

    def take_grads(mode):
        def wait_grad(member, from_core):
            arrival(
                mode.rows.at[1, member, rows16(from_core * BLOCK, BLOCK)],
                mode.grad_send.at[member],
                mode.grad_recv.at[member, from_core],
            ).wait_recv()

        def take(member):
            for from_core in range(2):
                wait_grad(member, from_core)
            add_tiles(mode, 1, member)

        wait_grad(mode.own_member, 1 - mode.core)
        add_tiles(mode, 1, mode.own_member)
        back_around(mode.members, mode.own_member, take)

    per_mode(take_grads)
    grad_out = sum_at_owners(1)
    grad_out_bf = grad_out.astype(BF)
    grad_normed = grad_out
    for h in range(2):
        grad_hidden = dot_nt(grad_out_bf, tall[0, h])
        value, slope = silu_parts(gate_keep[h])
        grad_up = (grad_hidden * value).astype(BF)
        grad_gate = (grad_hidden * up_keep[h] * slope).astype(BF)
        grad_normed = grad_normed + (dot_nt(grad_gate, wide[0, h]) + dot_nt(grad_up, wide[1, h]))
    sums = sum_keep[...]
    scale_basket = rms_scale(sums)
    inner_basket = jnp.sum(basket_gain * grad_normed * sums, axis=1, keepdims=True)
    cubed_basket = scale_basket * scale_basket * scale_basket
    grad_sum = scale_basket * basket_gain * grad_normed - sums * cubed_basket * inner_basket / D
    send_blocks(1, grad_sum.astype(BF))

    def back_copy(mode, member):
        return remote(
            mode.item_out.at[1, member],
            mode.back_in.at[mode.own_member],
            mode.back_send.at[member],
            mode.back_recv.at[mode.own_member],
            mode.item_shard(member),
            mode.core,
        )

    def finish(mode):
        pick_all(mode, 1)

        def send(member):
            mode.item_out[1, member] = dot(mode.spread[member], mode.picked[member]).astype(BF)
            back_copy(mode, member).start()

        around(mode.members, mode.own_member, send)
        mode.back_in[mode.own_member] = dot(
            mode.spread[mode.own_member], mode.picked[mode.own_member]
        ).astype(BF)

        def take(member):
            arrival(
                mode.back_in.at[member], mode.back_send.at[member], mode.back_recv.at[member]
            ).wait_recv()

        back_around(mode.members, mode.own_member, take)
        back = mode.back_in[0].astype(F32)
        for member in range(1, mode.members):
            back = back + mode.back_in[member].astype(F32)
        back_ref[...] = back

        def drain_member(member):
            words_copy(mode, member).wait_send()
            rows_copy(mode, member).wait_send()
            back_copy(mode, member).wait_send()
            for to_core in range(2):
                item_copy(mode, member, to_core).wait_send()

        around(mode.members, mode.own_member, drain_member)
        item_copy(mode, mode.own_member, 1 - mode.core).wait_send()

        def drain_column(column):
            for phase in range(2):
                for to_core in range(2):
                    owner_copy(mode, phase, column, to_core).wait_send()

        around(mode.columns, mode.own_column, drain_column)
        for phase in range(2):
            owner_copy(mode, phase, mode.own_column, 1 - mode.core).wait_send()

    per_mode(finish)

    for n in range(6):
        sibling_weight(n).wait_send()
    cot_copy().wait_send()
    for mode in modes:

        def drain_grad(member, mode=mode):
            grad_copy(mode, member).wait_send()

        def drain_block(column, mode=mode):
            for phase in range(2):
                block_copy(mode, phase, column).wait_send()

        around(mode.members, mode.own_member, drain_grad)
        around(mode.columns, mode.own_column, drain_block)

        @pl.when(m != mode.core)
        def _(mode=mode, drain_grad=drain_grad, drain_block=drain_block):
            drain_grad(mode.own_member)
            drain_block(mode.own_column)


def local(
    item_rows,
    first_moment,
    second_moment,
    item_cot,
    tile_bits,
    tile_item,
    tile_dest,
    basket_gain,
    item_gain,
    gate_basket,
    up_basket,
    down_basket,
    gate_item,
    up_item,
    down_item,
):
    vmem = pl.BlockSpec(memory_space=pltpu.VMEM)
    smem = pl.BlockSpec(memory_space=pltpu.SMEM)
    anywhere = pl.BlockSpec(memory_space=pltpu.HBM)
    back_items = pl.pallas_call(
        kernel,
        out_shape=jax.ShapeDtypeStruct((2 * BLOCK, HALF), F32),
        in_specs=[anywhere] * 3 + [smem, smem, vmem, vmem] + [anywhere] * 6,
        out_specs=vmem,
        scratch_shapes=[
            common_scratch(),
            mode_scratch(RING, PLANE),
            mode_scratch(PLANE, RING),
        ],
        compiler_params=pltpu.CompilerParams(
            collective_id=0, has_side_effects=True, vmem_limit_bytes=60 * 1024 * 1024
        ),
        name="layer",
    )(
        item_rows,
        item_cot,
        tile_bits,
        tile_item,
        tile_dest,
        basket_gain.reshape(1, D),
        item_gain.reshape(1, D),
        gate_basket,
        up_basket,
        down_basket,
        gate_item,
        up_item,
        down_item,
    )
    gradient = item_cot.astype(F32) + back_items
    new_first = BETA_FIRST * first_moment + (1.0 - BETA_FIRST) * gradient
    new_second = BETA_SECOND * second_moment + (1.0 - BETA_SECOND) * gradient * gradient
    new_rows = item_rows - LEARNING_RATE * new_first / (jnp.sqrt(new_second) + ADAM_EPSILON)
    return (new_rows, new_first, new_second)


def solution(mesh):
    split = P("shard", "mp")
    return jax.shard_map(
        local,
        mesh=mesh,
        in_specs=(
            split,
            split,
            split,
            split,
            P("shard", None, None),
            P("shard"),
            P("shard"),
            P(),
            P(),
            P(None, "mp"),
            P(None, "mp"),
            P("mp", None),
            P(None, "mp"),
            P(None, "mp"),
            P("mp", None),
        ),
        out_specs=(split, split, split),
        check_vma=False,
    )
```

time: 475 us -> 96.4 us (0.20)
  waiting for transfers between devices: 288 us -> 0 us
  Pallas kernels: 0 us -> 93.8 us
  blocking collectives: 69.1 us -> 0 us
  starting transfers between devices: 37.9 us -> 0 us
  other arithmetic: 33.9 us -> 1.69 us
  local copies, waits for them, and re-layouts: 17.5 us -> 0.02 us
  between operations: 14.6 us -> 0.71 us
  matrix products: 12.5 us -> 0 us
    all_to_all x3 -> x0, waiting for transfers between devices: 188 us -> none  [the longest x2 187 us: owner_sums(): lax.all_to_all(coalesced.astype(jnp.bfloat16), SHARD, split_axis=0, conca...]
    all_gather x2 -> x0, waiting for transfers between devices: 101 us -> none  [gather_axes(): value = lax.all_gather(value, axis, axis=dim, tiled=True)]
    pallas_call x0 -> x1, Pallas kernels: none -> 93.8 us  [local(): pl.pallas_call(kernel, out_shape=jax.ShapeDtypeStruct((2 * BLOCK, HALF),...]
    all_gather x4 -> x0, blocking collectives: 39.9 us -> none  [gather_axes(): value = lax.all_gather(value, axis, axis=dim, tiled=True)]
    all_to_all x3 -> x0, starting transfers between devices: 37.8 us -> none  [the longest x2 28.8 us: owner_sums(): lax.all_to_all(coalesced.astype(jnp.bfloat16), SHARD, split_axis=0, conca...]
    all_to_all x6 -> x0, blocking collectives: 29.1 us -> none  [the longest x5 25.3 us: sent_to_all(): return lax.all_to_all(copies, axis, split_axis=0, concat_axis=0, tiled=True)]
    convert_element_type x9 -> x0, other arithmetic: 15.1 us -> none  [the longest x2 12.7 us: owner_sums(): coalesced.astype(jnp.bfloat16)]
    dot_general x14 -> x0, matrix products: 12.5 us -> none  [the longest x1 2.13 us: local(): jnp.einsum('rh,dh->rd', grad_gate, gate_item, preferred_element_type=jnp....]
  transfers between devices with their start and end apart: 5 -> 0, of which waited for: 5 -> 0; matrix products, arithmetic and copies ran while one was open for 0% -> 0% of each run, Pallas kernels for 0% -> 0%
where the time goes in v2:
time: 96.4 us; the launch traced here: 96.2 us
  Pallas kernels  93.8 us (97%)
  other arithmetic  1.69 us (2%)
    pallas_call x1, Pallas kernels, local(): pl.pallas_call(kernel, out_shape=jax.ShapeDtypeStruct((2 * BLOCK, HALF),...  93.8 us

profile of v2, /device:TPU:1, one launch (start us, length us, event | category | flops | bytes accessed | tf_op | source)
XLA Modules:
  0.0 96.2 jit_solution(17271106920110517066)
XLA Ops:
  0.6 0.0 copy-start
  0.6 0.0 copy-start.1
  0.7 0.0 copy-start.2
  0.7 0.0 copy-start.3
  0.7 93.8 %layer.1 = f32[256,128]{1,0:T(8,128)} custom-call(f32[256,128]{1,0:T(8,128)} %rows_hbm.1, bf16[256,128]{1,0:T(8,128)(2,1)} %cot_hbm.1, s32[16,8,128]{2,1,0:T(8,128)} %bits_hbm.1, s32[16]{0:T(128)} %item_ref.1, s32[16]{0:T(128)} %dest_ref.1, f32[1,256]{1,0:T(1,128)} %bitcast.2, f32[1,256]{1,0:T(1,128)} %bitcast.3, bf16[256,1024]{1,0:T(8,128)(2,1)} %gate_b_ref.1, ...), custom_call_target="tpu_custom_call" | custom-call | tf_op jit(solution)/shard_map/layer/pallas_call | solution.py:759
  94.5 0.0 copy-done
  94.5 0.0 copy-done.1
  94.5 0.0 copy-done.2
  94.5 0.0 copy-done.3
  94.5 1.7 %divide_subtract_fusion = (f32[256,128]{1,0:T(8,128)}, f32[256,128]{1,0:T(8,128)}, f32[256,128]{1,0:T(8,128)}) fusion(f32[256,128]{1,0:T(8,128)S(1)} %copy-done, f32[256,128]{1,0:T(8,128)} %layer.1, bf16[256,128]{1,0:T(8,128)(2,1)S(1)} %copy-done.1, f32[256,128]{1,0:T(8,128)S(1)} %copy-done.2, f32[256,128]{1,0:T(8,128)S(1)} %copy-done.3), kind=kLoop, calls=%fused_computation.2 | loop fusion | flops 425984 | bytes 983040 | tf_op jit(solution)/shard_map/sub | solution.py:791
Async XLA Ops:
  0.6 93.9 %copy-start = (f32[256,128]{1,0:T(8,128)S(1)}, f32[256,128]{1,0:T(8,128)}, u32[]{:S(2)}) copy-start(f32[256,128]{1,0:T(8,128)} %rows_hbm.1) | copy-start | bytes 393220
  0.6 93.9 %copy-start.1 = (bf16[256,128]{1,0:T(8,128)(2,1)S(1)}, bf16[256,128]{1,0:T(8,128)(2,1)}, u32[]{:S(2)}) copy-start(bf16[256,128]{1,0:T(8,128)(2,1)} %cot_hbm.1) | copy-start | bytes 196612
  0.7 93.9 %copy-start.2 = (f32[256,128]{1,0:T(8,128)S(1)}, f32[256,128]{1,0:T(8,128)}, u32[]{:S(2)}) copy-start(f32[256,128]{1,0:T(8,128)} %param.16) | copy-start | bytes 393220
  0.7 93.9 %copy-start.3 = (f32[256,128]{1,0:T(8,128)S(1)}, f32[256,128]{1,0:T(8,128)}, u32[]{:S(2)}) copy-start(f32[256,128]{1,0:T(8,128)} %param.17) | copy-start | bytes 393220

commit v3 on v2

--- a/solution.py
+++ b/solution.py
@@ -11,6 +11,7 @@
 TILE_DEV = 16
 RING = 8
 PLANE = 16
+PARTS = RING + PLANE
 OWN = 64
 HIDDEN = 1024
 
@@ -47,7 +48,6 @@
 
 
 def mode_scratch(members, columns):
-    dma = pltpu.SemaphoreType.DMA
     wide = TILE_DEV * columns
     tiles = TILE_DEV * members
     slots = wide // 128 + 1
@@ -60,29 +60,13 @@
         "select_cols": pltpu.VMEM((BLOCK, 2 * tiles), BF),
         "select_rows": pltpu.VMEM((tiles, BLOCK), BF),
         "tile_sums": pltpu.VMEM((columns, 2 * tiles, HALF), BF),
-        "owner_out": pltpu.VMEM((2, columns, BLOCK, HALF), BF),
-        "owner_in": pltpu.VMEM((2, columns, OWN, HALF), BF),
+        "owner_out": pltpu.VMEM((2, 2 * columns, OWN, HALF), BF),
         "block_out": pltpu.VMEM((2, OWN, HALF), BF),
         "block_in": pltpu.VMEM((2, columns, BLOCK, HALF), BF),
         "picked": pltpu.VMEM((members, wide, HALF), BF),
-        "item_out": pltpu.VMEM((2, members, 2 * BLOCK, HALF), BF),
-        "item_in": pltpu.VMEM((members, BLOCK, HALF), BF),
-        "back_in": pltpu.VMEM((members, 2 * BLOCK, HALF), BF),
+        "item_out": pltpu.VMEM((2, 2 * members, BLOCK, HALF), BF),
+        "back_in": pltpu.VMEM((members, 2, BLOCK, HALF), BF),
         "grad_out": pltpu.VMEM((BLOCK, HALF), BF),
-        "words_send": dma((members,)),
-        "words_recv": dma((members,)),
-        "rows_send": dma((members,)),
-        "rows_recv": dma((members,)),
-        "owner_send": dma((2, columns, 2)),
-        "owner_recv": dma((2, columns)),
-        "block_send": dma((2, columns)),
-        "block_recv": dma((2, columns, 2)),
-        "item_send": dma((members, 2)),
-        "item_recv": dma((members,)),
-        "grad_send": dma((members,)),
-        "grad_recv": dma((members, 2)),
-        "back_send": dma((members,)),
-        "back_recv": dma((members,)),
     }
 
 
@@ -103,6 +87,22 @@
         "weight_recv": dma((6,)),
         "cot_send": dma,
         "cot_recv": dma,
+        "owner_in": pltpu.VMEM((2, PARTS, OWN, HALF), BF),
+        "item_in": pltpu.VMEM((PARTS, BLOCK, HALF), BF),
+        "words_send": dma,
+        "words_recv": dma,
+        "rows_send": dma,
+        "rows_recv": dma((PLANE,)),
+        "owner_send": dma((2,)),
+        "owner_recv": dma((2,)),
+        "block_send": dma((2,)),
+        "block_recv": dma((2, PLANE)),
+        "item_send": dma,
+        "item_recv": dma,
+        "grad_send": dma,
+        "grad_recv": dma((PLANE,)),
+        "back_send": dma,
+        "back_recv": dma,
     }
 
 
@@ -111,6 +111,8 @@
         self.core = core
         self.members, self.columns = (RING, PLANE) if core == 0 else (PLANE, RING)
         self.own_member, self.own_column = (z, q) if core == 0 else (q, z)
+        self.first = 0 if core == 0 else PLANE
+        self.first_item = 0 if core == 0 else RING
         self.z, self.q = z, q
         self.__dict__.update(refs)
 
@@ -153,6 +155,14 @@
     weight_own, weight_send = common["weight_own"], common["weight_send"]
     weight_recv = common["weight_recv"]
     cot_send, cot_recv = common["cot_send"], common["cot_recv"]
+    owner_in, item_in = common["owner_in"], common["item_in"]
+    words_send, words_recv = common["words_send"], common["words_recv"]
+    rows_send, rows_recv = common["rows_send"], common["rows_recv"]
+    owner_send, owner_recv = common["owner_send"], common["owner_recv"]
+    block_send, block_recv = common["block_send"], common["block_recv"]
+    item_send, item_recv = common["item_send"], common["item_recv"]
+    grad_send, grad_recv = common["grad_send"], common["grad_recv"]
+    back_send, back_recv = common["back_send"], common["back_recv"]
 
     def remote(src, dst, send, recv, to_shard, to_core):
         return pltpu.make_async_remote_copy(
@@ -164,8 +174,11 @@
             device_id_type=MESH,
         )
 
-    def arrival(dst, send, recv):
-        return remote(dst, dst, send, recv, shard, other)
+    def arrived(ref, recv):
+        remote(ref, ref, cot_send, recv, shard, other).wait_recv()
+
+    def sent(ref, send):
+        remote(ref, ref, send, cot_recv, shard, other).wait_send()
 
     def around(count, own, body):
         def step(n, carry):
@@ -283,8 +296,8 @@
         return remote(
             mode.words_out.at[member],
             mode.words_in.at[mode.own_member],
-            mode.words_send.at[member],
-            mode.words_recv.at[mode.own_member],
+            words_send,
+            words_recv,
             mode.item_shard(member),
             mode.core,
         )
@@ -293,8 +306,8 @@
         return remote(
             mode.rows.at[0, mode.own_member],
             mode.rows.at[0, mode.own_member],
-            mode.rows_send.at[member],
-            mode.rows_recv.at[mode.own_member],
+            rows_send,
+            rows_recv.at[mode.own_member],
             mode.item_shard(member),
             mode.core,
         )
@@ -361,16 +374,9 @@
             mode.spread[member] = dot(mat, to_columns).astype(BF)
             mode.collect[member] = dot_nt(from_tiles, mat).astype(BF)
 
-        def take_words(member):
-            arrival(
-                mode.words_in.at[member],
-                mode.words_send.at[member],
-                mode.words_recv.at[member],
-            ).wait_recv()
-            unpack(member)
-
         unpack(mode.own_member)
-        back_around(mode.members, mode.own_member, take_words)
+        arrived(mode.words_in.at[: mode.members - 1], words_recv)
+        back_around(mode.members, mode.own_member, unpack)
 
         tiles = TILE_DEV * mode.members
         about = mode.words_in[0, slots]
@@ -392,9 +398,7 @@
         add_tiles(mode, 0, mode.own_member)
 
         def take(member):
-            arrival(
-                mode.rows.at[0, member], mode.rows_send.at[member], mode.rows_recv.at[member]
-            ).wait_recv()
+            arrived(mode.rows.at[0, member], rows_recv.at[member])
             add_tiles(mode, 0, member)
 
         back_around(mode.members, mode.own_member, take)
@@ -403,19 +407,18 @@
 
     def owner_copy(mode, phase, column, to_core):
         return remote(
-            mode.owner_out.at[phase, column, rows16(to_core * OWN, OWN)],
-            mode.owner_in.at[phase, mode.own_column],
-            mode.owner_send.at[phase, column, to_core],
-            mode.owner_recv.at[phase, mode.own_column],
+            mode.owner_out.at[phase, 2 * column + to_core],
+            owner_in.at[phase, mode.first + mode.own_column],
+            owner_send.at[phase],
+            owner_recv.at[phase],
             mode.basket_shard(column),
             to_core,
         )
 
     def send_sums(mode, phase):
         def column_sum(column):
-            mode.owner_out[phase, column] = dot(
-                mode.select_cols[...], mode.tile_sums[column]
-            ).astype(BF)
+            total = dot(mode.select_cols[...], mode.tile_sums[column]).astype(BF)
+            mode.owner_out[phase, pl.ds(2 * column, 2)] = total.reshape(2, OWN, HALF)
 
         def send(column):
             column_sum(column)
@@ -425,32 +428,18 @@
         around(mode.columns, mode.own_column, send)
         column_sum(mode.own_column)
         owner_copy(mode, phase, mode.own_column, 1 - mode.core).start()
-        mode.owner_in[phase, mode.own_column] = mode.owner_out[
-            phase, mode.own_column, mode.core * OWN : (mode.core + 1) * OWN, :
+        owner_in[phase, mode.first + mode.own_column] = mode.owner_out[
+            phase, 2 * mode.own_column + mode.core
         ]
 
     def sum_at_owners(phase):
         per_mode(lambda mode: send_sums(mode, phase))
-        for mode in modes:
-
-            def take(column, mode=mode):
-                arrival(
-                    mode.owner_in.at[phase, column],
-                    mode.owner_send.at[phase, column, 0],
-                    mode.owner_recv.at[phase, column],
-                ).wait_recv()
-
-            back_around(mode.columns, mode.own_column, take)
-
-            @pl.when(m != mode.core)
-            def _(mode=mode, take=take):
-                take(mode.own_column)
-
+        arrived(owner_in.at[phase, : PARTS - 1], owner_recv.at[phase])
         halves = []
         for mode in modes:
-            total = mode.owner_in[phase, 0].astype(F32)
+            total = owner_in[phase, mode.first].astype(F32)
             for column in range(1, mode.columns):
-                total = total + mode.owner_in[phase, column].astype(F32)
+                total = total + owner_in[phase, mode.first + column].astype(F32)
             halves.append(total)
         return jnp.concatenate(halves, axis=1)
 
@@ -458,8 +447,8 @@
         return remote(
             mode.block_out.at[phase],
             mode.block_in.at[phase, mode.own_column, rows16(m * OWN, OWN)],
-            mode.block_send.at[phase, column],
-            mode.block_recv.at[phase, mode.own_column, m],
+            block_send.at[phase],
+            block_recv.at[phase, mode.own_column],
             mode.basket_shard(column),
             mode.core,
         )
@@ -483,13 +472,6 @@
             def _(mode=mode):
                 place = slice(mode.core * OWN, (mode.core + 1) * OWN)
                 mode.block_in[phase, mode.own_column, place, :] = mode.block_out[phase]
-
-    def wait_block(mode, phase, column, from_core):
-        arrival(
-            mode.block_in.at[phase, column, rows16(from_core * OWN, OWN)],
-            mode.block_send.at[phase, column],
-            mode.block_recv.at[phase, column, from_core],
-        ).wait_recv()
 
     def pick_all(mode, phase):
         def pick(column):
@@ -499,11 +481,12 @@
             )
 
         def take(column):
-            for from_core in range(2):
-                wait_block(mode, phase, column, from_core)
+            arrived(mode.block_in.at[phase, column], block_recv.at[phase, column])
             pick(column)
 
-        wait_block(mode, phase, mode.own_column, 1 - mode.core)
+        arrived(
+            mode.block_in.at[phase, mode.own_column, :OWN], block_recv.at[phase, mode.own_column]
+        )
         pick(mode.own_column)
         back_around(mode.columns, mode.own_column, take)
 
@@ -529,10 +512,10 @@
 
     def item_copy(mode, member, to_core):
         return remote(
-            mode.item_out.at[0, member, rows16(to_core * BLOCK, BLOCK)],
-            mode.item_in.at[mode.own_member],
-            mode.item_send.at[member, to_core],
-            mode.item_recv.at[mode.own_member],
+            mode.item_out.at[0, 2 * member + to_core],
+            item_in.at[mode.first_item + mode.own_member],
+            item_send,
+            item_recv,
             mode.item_shard(member),
             to_core,
         )
@@ -541,7 +524,8 @@
         pick_all(mode, 0)
 
         def partial(member):
-            mode.item_out[0, member] = dot(mode.spread[member], mode.picked[member]).astype(BF)
+            total = dot(mode.spread[member], mode.picked[member]).astype(BF)
+            mode.item_out[0, pl.ds(2 * member, 2)] = total.reshape(2, BLOCK, HALF)
 
         def send(member):
             partial(member)
@@ -551,8 +535,8 @@
         around(mode.members, mode.own_member, send)
         partial(mode.own_member)
         item_copy(mode, mode.own_member, 1 - mode.core).start()
-        mode.item_in[mode.own_member] = mode.item_out[
-            0, mode.own_member, mode.core * BLOCK : (mode.core + 1) * BLOCK, :
+        item_in[mode.first_item + mode.own_member] = mode.item_out[
+            0, 2 * mode.own_member + mode.core
         ]
 
     per_mode(send_items)
@@ -560,26 +544,14 @@
     for n in range(3, 6):
         own_weight(n).wait()
         sibling_weight(n).wait_recv()
-    arrival(cot_whole.at[other], cot_send, cot_recv).wait_recv()
+    arrived(cot_whole.at[other], cot_recv)
     load_cot.wait()
-    for mode in modes:
-
-        def take_item(member, mode=mode):
-            arrival(
-                mode.item_in.at[member], mode.item_send.at[member, 0], mode.item_recv.at[member]
-            ).wait_recv()
-
-        back_around(mode.members, mode.own_member, take_item)
-
-        @pl.when(m != mode.core)
-        def _(mode=mode, take_item=take_item):
-            take_item(mode.own_member)
-
+    arrived(item_in.at[: PARTS - 1], item_recv)
     halves = []
     for mode in modes:
-        summed = mode.item_in[0].astype(F32)
+        summed = item_in[mode.first_item].astype(F32)
         for member in range(1, mode.members):
-            summed = summed + mode.item_in[member].astype(F32)
+            summed = summed + item_in[mode.first_item + member].astype(F32)
         halves.append(summed)
     message = jnp.concatenate(halves, axis=1)
     cot_full = jnp.concatenate([cot_whole[0], cot_whole[1]], axis=1)
@@ -602,8 +574,8 @@
         return remote(
             mode.grad_out,
             mode.rows.at[1, mode.own_member, rows16(m * BLOCK, BLOCK)],
-            mode.grad_send.at[member],
-            mode.grad_recv.at[mode.own_member, m],
+            grad_send,
+            grad_recv.at[mode.own_member],
             mode.item_shard(member),
             mode.core,
         )
@@ -628,19 +600,11 @@
             mode.rows[1, mode.own_member, place, :] = mode.grad_out[...]
 
     def take_grads(mode):
-        def wait_grad(member, from_core):
-            arrival(
-                mode.rows.at[1, member, rows16(from_core * BLOCK, BLOCK)],
-                mode.grad_send.at[member],
-                mode.grad_recv.at[member, from_core],
-            ).wait_recv()
-
         def take(member):
-            for from_core in range(2):
-                wait_grad(member, from_core)
+            arrived(mode.rows.at[1, member], grad_recv.at[member])
             add_tiles(mode, 1, member)
 
-        wait_grad(mode.own_member, 1 - mode.core)
+        arrived(mode.rows.at[1, mode.own_member, :BLOCK], grad_recv.at[mode.own_member])
         add_tiles(mode, 1, mode.own_member)
         back_around(mode.members, mode.own_member, take)
 
@@ -663,10 +627,10 @@
 
     def back_copy(mode, member):
         return remote(
-            mode.item_out.at[1, member],
+            mode.item_out.at[1, pl.ds(2 * member, 2)],
             mode.back_in.at[mode.own_member],
-            mode.back_send.at[member],
-            mode.back_recv.at[mode.own_member],
+            back_send,
+            back_recv,
             mode.item_shard(member),
             mode.core,
         )
@@ -674,66 +638,36 @@
     def finish(mode):
         pick_all(mode, 1)
 
+        def partial(member):
+            total = dot(mode.spread[member], mode.picked[member]).astype(BF)
+            return total.reshape(2, BLOCK, HALF)
+
         def send(member):
-            mode.item_out[1, member] = dot(mode.spread[member], mode.picked[member]).astype(BF)
+            mode.item_out[1, pl.ds(2 * member, 2)] = partial(member)
             back_copy(mode, member).start()
 
         around(mode.members, mode.own_member, send)
-        mode.back_in[mode.own_member] = dot(
-            mode.spread[mode.own_member], mode.picked[mode.own_member]
-        ).astype(BF)
-
-        def take(member):
-            arrival(
-                mode.back_in.at[member], mode.back_send.at[member], mode.back_recv.at[member]
-            ).wait_recv()
-
-        back_around(mode.members, mode.own_member, take)
-        back = mode.back_in[0].astype(F32)
-        for member in range(1, mode.members):
-            back = back + mode.back_in[member].astype(F32)
-        back_ref[...] = back
-
-        def drain_member(member):
-            words_copy(mode, member).wait_send()
-            rows_copy(mode, member).wait_send()
-            back_copy(mode, member).wait_send()
-            for to_core in range(2):
-                item_copy(mode, member, to_core).wait_send()
-
-        around(mode.members, mode.own_member, drain_member)
-        item_copy(mode, mode.own_member, 1 - mode.core).wait_send()
-
-        def drain_column(column):
-            for phase in range(2):
-                for to_core in range(2):
-                    owner_copy(mode, phase, column, to_core).wait_send()
-
-        around(mode.columns, mode.own_column, drain_column)
+        mode.back_in[mode.own_member] = partial(mode.own_member)
+        sent(mode.words_out.at[: mode.members - 1], words_send)
+        sent(mode.rows.at[0, : mode.members - 1], rows_send)
+        sent(mode.item_out.at[0, : 2 * mode.members - 1], item_send)
         for phase in range(2):
-            owner_copy(mode, phase, mode.own_column, 1 - mode.core).wait_send()
+            sent(mode.owner_out.at[phase, : 2 * mode.columns - 1], owner_send.at[phase])
+            sent(owner_in.at[phase, : PARTS - 1], block_send.at[phase])
+        sent(item_in.at[: PARTS - 1], grad_send)
+        arrived(mode.back_in.at[: mode.members - 1], back_recv)
+        for block in range(2):
+            back = mode.back_in[0, block].astype(F32)
+            for member in range(1, mode.members):
+                back = back + mode.back_in[member, block].astype(F32)
+            back_ref[block * BLOCK : (block + 1) * BLOCK, :] = back
+        sent(mode.back_in.at[: mode.members - 1], back_send)
 
     per_mode(finish)
 
     for n in range(6):
         sibling_weight(n).wait_send()
     cot_copy().wait_send()
-    for mode in modes:
-
-        def drain_grad(member, mode=mode):
-            grad_copy(mode, member).wait_send()
-
-        def drain_block(column, mode=mode):
-            for phase in range(2):
-                block_copy(mode, phase, column).wait_send()
-
-        around(mode.members, mode.own_member, drain_grad)
-        around(mode.columns, mode.own_column, drain_block)
-
-        @pl.when(m != mode.core)
-        def _(mode=mode, drain_grad=drain_grad, drain_block=drain_block):
-            drain_grad(mode.own_member)
-            drain_block(mode.own_column)
 
 
 def local(

time: 96.4 us -> 90.6 us (0.940)
  Pallas kernels: 93.8 us -> 88.1 us
    pallas_call x1, Pallas kernels: 93.8 us -> 88.1 us  [local(): pl.pallas_call(kernel, out_shape=jax.ShapeDtypeStruct((2 * BLOCK, HALF),...]
where the time goes in v3:
time: 90.6 us; the launch traced here: 90.5 us
  Pallas kernels  88.1 us (97%)
  other arithmetic  1.69 us (2%)
    pallas_call x1, Pallas kernels, local(): pl.pallas_call(kernel, out_shape=jax.ShapeDtypeStruct((2 * BLOCK, HALF),...  88.1 us

profile of v3, /device:TPU:1, one launch (start us, length us, event | category | flops | bytes accessed | tf_op | source)
XLA Modules:
  0.0 90.5 jit_solution(8800733997125064123)
XLA Ops:
  0.6 0.0 copy-start
  0.6 0.0 copy-start.1
  0.7 0.0 copy-start.2
  0.7 0.0 copy-start.3
  0.7 88.1 %layer.1 = f32[256,128]{1,0:T(8,128)} custom-call(f32[256,128]{1,0:T(8,128)} %rows_hbm.1, bf16[256,128]{1,0:T(8,128)(2,1)} %cot_hbm.1, s32[16,8,128]{2,1,0:T(8,128)} %bits_hbm.1, s32[16]{0:T(128)} %item_ref.1, s32[16]{0:T(128)} %dest_ref.1, f32[1,256]{1,0:T(1,128)} %bitcast.2, f32[1,256]{1,0:T(1,128)} %bitcast.3, bf16[256,1024]{1,0:T(8,128)(2,1)} %gate_b_ref.1, ...), custom_call_target="tpu_custom_call" | custom-call | tf_op jit(solution)/shard_map/layer/pallas_call | solution.py:693
  88.8 0.0 copy-done
  88.8 0.0 copy-done.1
  88.8 0.0 copy-done.2
  88.8 0.0 copy-done.3
  88.8 1.7 %divide_subtract_fusion = (f32[256,128]{1,0:T(8,128)}, f32[256,128]{1,0:T(8,128)}, f32[256,128]{1,0:T(8,128)}) fusion(f32[256,128]{1,0:T(8,128)S(1)} %copy-done, f32[256,128]{1,0:T(8,128)} %layer.1, bf16[256,128]{1,0:T(8,128)(2,1)S(1)} %copy-done.1, f32[256,128]{1,0:T(8,128)S(1)} %copy-done.2, f32[256,128]{1,0:T(8,128)S(1)} %copy-done.3), kind=kLoop, calls=%fused_computation.2 | loop fusion | flops 425984 | bytes 983040 | tf_op jit(solution)/shard_map/sub | solution.py:725
Async XLA Ops:
  0.6 88.1 %copy-start = (f32[256,128]{1,0:T(8,128)S(1)}, f32[256,128]{1,0:T(8,128)}, u32[]{:S(2)}) copy-start(f32[256,128]{1,0:T(8,128)} %rows_hbm.1) | copy-start | bytes 393220
  0.6 88.1 %copy-start.1 = (bf16[256,128]{1,0:T(8,128)(2,1)S(1)}, bf16[256,128]{1,0:T(8,128)(2,1)}, u32[]{:S(2)}) copy-start(bf16[256,128]{1,0:T(8,128)(2,1)} %cot_hbm.1) | copy-start | bytes 196612
  0.7 88.1 %copy-start.2 = (f32[256,128]{1,0:T(8,128)S(1)}, f32[256,128]{1,0:T(8,128)}, u32[]{:S(2)}) copy-start(f32[256,128]{1,0:T(8,128)} %param.16) | copy-start | bytes 393220
  0.7 88.1 %copy-start.3 = (f32[256,128]{1,0:T(8,128)S(1)}, f32[256,128]{1,0:T(8,128)}, u32[]{:S(2)}) copy-start(f32[256,128]{1,0:T(8,128)} %param.17) | copy-start | bytes 393220

commit v4 on v3

--- a/solution.py
+++ b/solution.py
@@ -187,12 +187,37 @@
 
         lax.fori_loop(1, count, step, 0)
 
-    def back_around(count, own, body):
+    def ahead(count, own, size, work, send, send_own):
+        def group(n, last):
+            places = [lax.rem(own + n * size + i + 1, count) for i in range(size)]
+            work(places)
+            for place in places[: size - 1] if last else places:
+                send(place)
+            if last:
+                send_own()
+
         def step(n, carry):
-            body(lax.rem(own + count - n, count))
+            group(n, False)
             return carry
 
-        lax.fori_loop(1, count, step, 0)
+        lax.fori_loop(0, count // size - 1, step, 0)
+        group(count // size - 1, True)
+
+    def behind(count, own, size, wait_own, wait, work):
+        def group(n, first):
+            places = [lax.rem(own + count - n * size - i, count) for i in range(size)]
+            if first:
+                wait_own()
+            for place in places[1:] if first else places:
+                wait(place)
+            work(places)
+
+        def step(n, carry):
+            group(n, False)
+            return carry
+
+        group(0, True)
+        lax.fori_loop(1, count // size, step, 0)
 
     def per_mode(body):
         for mode in modes:
@@ -334,14 +359,15 @@
     for n in range(3, 6):
         sibling_weight(n).start()
 
-    def add_tiles(mode, phase, member):
-        sums = dot(mode.collect[member], mode.rows[phase, member])
-        high = sums.astype(BF)
-        low = (sums - high.astype(F32)).astype(BF)
+    def add_tiles(mode, phase, members):
+        all_sums = [dot(mode.collect[member], mode.rows[phase, member]) for member in members]
         shape = (mode.columns, TILE_DEV, HALF)
         tiles = TILE_DEV * mode.members
-        mode.tile_sums[:, rows16(member * TILE_DEV, TILE_DEV), :] = high.reshape(shape)
-        mode.tile_sums[:, rows16(tiles + member * TILE_DEV, TILE_DEV), :] = low.reshape(shape)
+        for member, sums in zip(members, all_sums):
+            high = sums.astype(BF)
+            low = (sums - high.astype(F32)).astype(BF)
+            mode.tile_sums[:, rows16(member * TILE_DEV, TILE_DEV), :] = high.reshape(shape)
+            mode.tile_sums[:, rows16(tiles + member * TILE_DEV, TILE_DEV), :] = low.reshape(shape)
 
     def take_rows(mode):
         size = TILE_DEV * mode.columns
@@ -374,9 +400,13 @@
             mode.spread[member] = dot(mat, to_columns).astype(BF)
             mode.collect[member] = dot_nt(from_tiles, mat).astype(BF)
 
-        unpack(mode.own_member)
+        def unpack_pair(n, carry):
+            for i in range(2):
+                unpack(2 * n + i)
+            return carry
+
         arrived(mode.words_in.at[: mode.members - 1], words_recv)
-        back_around(mode.members, mode.own_member, unpack)
+        lax.fori_loop(0, mode.members // 2, unpack_pair, 0)
 
         tiles = TILE_DEV * mode.members
         about = mode.words_in[0, slots]
@@ -395,13 +425,14 @@
             eye, one_hot, (((1,), (1,)), ((), ())), preferred_element_type=F32
         ).astype(BF)
 
-        add_tiles(mode, 0, mode.own_member)
-
-        def take(member):
-            arrived(mode.rows.at[0, member], rows_recv.at[member])
-            add_tiles(mode, 0, member)
-
-        back_around(mode.members, mode.own_member, take)
+        behind(
+            mode.members,
+            mode.own_member,
+            2,
+            lambda: None,
+            lambda member: arrived(mode.rows.at[0, member], rows_recv.at[member]),
+            lambda members: add_tiles(mode, 0, members),
+        )
 
     per_mode(take_rows)
 
@@ -416,18 +447,23 @@
         )
 
     def send_sums(mode, phase):
-        def column_sum(column):
-            total = dot(mode.select_cols[...], mode.tile_sums[column]).astype(BF)
-            mode.owner_out[phase, pl.ds(2 * column, 2)] = total.reshape(2, OWN, HALF)
+        def column_sums(columns):
+            for k in range(0, len(columns), 2):
+                pair = jnp.concatenate([mode.tile_sums[c] for c in columns[k : k + 2]], axis=1)
+                total = dot(mode.select_cols[...], pair).astype(BF)
+                for i, column in enumerate(columns[k : k + 2]):
+                    mode.owner_out[phase, pl.ds(2 * column, 2)] = total[
+                        :, i * HALF : (i + 1) * HALF
+                    ].reshape(2, OWN, HALF)
 
         def send(column):
-            column_sum(column)
             for to_core in range(2):
                 owner_copy(mode, phase, column, to_core).start()
 
-        around(mode.columns, mode.own_column, send)
-        column_sum(mode.own_column)
-        owner_copy(mode, phase, mode.own_column, 1 - mode.core).start()
+        def send_own():
+            owner_copy(mode, phase, mode.own_column, 1 - mode.core).start()
+
+        ahead(mode.columns, mode.own_column, 4, column_sums, send, send_own)
         owner_in[phase, mode.first + mode.own_column] = mode.owner_out[
             phase, 2 * mode.own_column + mode.core
         ]
@@ -474,21 +510,28 @@
                 mode.block_in[phase, mode.own_column, place, :] = mode.block_out[phase]
 
     def pick_all(mode, phase):
-        def pick(column):
-            chosen = dot(mode.select_rows[...], mode.block_in[phase, column]).astype(BF)
-            mode.picked[:, rows16(column * TILE_DEV, TILE_DEV), :] = chosen.reshape(
-                mode.members, TILE_DEV, HALF
-            )
-
-        def take(column):
-            arrived(mode.block_in.at[phase, column], block_recv.at[phase, column])
-            pick(column)
-
-        arrived(
-            mode.block_in.at[phase, mode.own_column, :OWN], block_recv.at[phase, mode.own_column]
-        )
-        pick(mode.own_column)
-        back_around(mode.columns, mode.own_column, take)
+        def pick(columns):
+            for k in range(0, len(columns), 2):
+                pair = jnp.concatenate(
+                    [mode.block_in[phase, c] for c in columns[k : k + 2]], axis=1
+                )
+                chosen = dot(mode.select_rows[...], pair).astype(BF)
+                for i, column in enumerate(columns[k : k + 2]):
+                    mode.picked[:, rows16(column * TILE_DEV, TILE_DEV), :] = chosen[
+                        :, i * HALF : (i + 1) * HALF
+                    ].reshape(mode.members, TILE_DEV, HALF)
+
+        behind(
+            mode.columns,
+            mode.own_column,
+            4,
+            lambda: arrived(
+                mode.block_in.at[phase, mode.own_column, :OWN],
+                block_recv.at[phase, mode.own_column],
+            ),
+            lambda column: arrived(mode.block_in.at[phase, column], block_recv.at[phase, column]),
+            pick,
+        )
 
     basket_gain = gain_b_ref[...]
     item_gain = gain_i_ref[...]
@@ -523,18 +566,19 @@
     def send_items(mode):
         pick_all(mode, 0)
 
-        def partial(member):
-            total = dot(mode.spread[member], mode.picked[member]).astype(BF)
-            mode.item_out[0, pl.ds(2 * member, 2)] = total.reshape(2, BLOCK, HALF)
+        def partials(members):
+            totals = [dot(mode.spread[member], mode.picked[member]) for member in members]
+            for member, total in zip(members, totals):
+                mode.item_out[0, pl.ds(2 * member, 2)] = total.astype(BF).reshape(2, BLOCK, HALF)
 
         def send(member):
-            partial(member)
             for to_core in range(2):
                 item_copy(mode, member, to_core).start()
 
-        around(mode.members, mode.own_member, send)
-        partial(mode.own_member)
-        item_copy(mode, mode.own_member, 1 - mode.core).start()
+        def send_own():
+            item_copy(mode, mode.own_member, 1 - mode.core).start()
+
+        ahead(mode.members, mode.own_member, 2, partials, send, send_own)
         item_in[mode.first_item + mode.own_member] = mode.item_out[
             0, 2 * mode.own_member + mode.core
         ]
@@ -600,13 +644,16 @@
             mode.rows[1, mode.own_member, place, :] = mode.grad_out[...]
 
     def take_grads(mode):
-        def take(member):
-            arrived(mode.rows.at[1, member], grad_recv.at[member])
-            add_tiles(mode, 1, member)
-
-        arrived(mode.rows.at[1, mode.own_member, :BLOCK], grad_recv.at[mode.own_member])
-        add_tiles(mode, 1, mode.own_member)
-        back_around(mode.members, mode.own_member, take)
+        behind(
+            mode.members,
+            mode.own_member,
+            2,
+            lambda: arrived(
+                mode.rows.at[1, mode.own_member, :BLOCK], grad_recv.at[mode.own_member]
+            ),
+            lambda member: arrived(mode.rows.at[1, member], grad_recv.at[member]),
+            lambda members: add_tiles(mode, 1, members),
+        )
 
     per_mode(take_grads)
     grad_out = sum_at_owners(1)
@@ -638,16 +685,20 @@
     def finish(mode):
         pick_all(mode, 1)
 
-        def partial(member):
-            total = dot(mode.spread[member], mode.picked[member]).astype(BF)
-            return total.reshape(2, BLOCK, HALF)
-
-        def send(member):
-            mode.item_out[1, pl.ds(2 * member, 2)] = partial(member)
-            back_copy(mode, member).start()
-
-        around(mode.members, mode.own_member, send)
-        mode.back_in[mode.own_member] = partial(mode.own_member)
+        def partials(members):
+            totals = [dot(mode.spread[member], mode.picked[member]) for member in members]
+            for member, total in zip(members, totals):
+                mode.item_out[1, pl.ds(2 * member, 2)] = total.astype(BF).reshape(2, BLOCK, HALF)
+
+        ahead(
+            mode.members,
+            mode.own_member,
+            2,
+            partials,
+            lambda member: back_copy(mode, member).start(),
+            lambda: None,
+        )
+        mode.back_in[mode.own_member] = mode.item_out[1, pl.ds(2 * mode.own_member, 2)]
         sent(mode.words_out.at[: mode.members - 1], words_send)
         sent(mode.rows.at[0, : mode.members - 1], rows_send)
         sent(mode.item_out.at[0, : 2 * mode.members - 1], item_send)

time: 90.6 us -> 87.1 us (0.961)
  Pallas kernels: 88.1 us -> 84.4 us
    pallas_call x1, Pallas kernels: 88.1 us -> 84.4 us  [local(): pl.pallas_call(kernel, out_shape=jax.ShapeDtypeStruct((2 * BLOCK, HALF),...]
where the time goes in v4:
time: 87.1 us; the launch traced here: 86.8 us
  Pallas kernels  84.4 us (97%)
  other arithmetic  1.69 us (2%)
    pallas_call x1, Pallas kernels, local(): pl.pallas_call(kernel, out_shape=jax.ShapeDtypeStruct((2 * BLOCK, HALF),...  84.4 us

profile of v4, /device:TPU:1, one launch (start us, length us, event | category | flops | bytes accessed | tf_op | source)
XLA Modules:
  0.0 86.8 jit_solution(3141939028796761260)
XLA Ops:
  0.6 0.0 copy-start
  0.6 0.0 copy-start.1
  0.7 0.0 copy-start.2
  0.7 0.0 copy-start.3
  0.7 84.4 %layer.1 = f32[256,128]{1,0:T(8,128)} custom-call(f32[256,128]{1,0:T(8,128)} %rows_hbm.1, bf16[256,128]{1,0:T(8,128)(2,1)} %cot_hbm.1, s32[16,8,128]{2,1,0:T(8,128)} %bits_hbm.1, s32[16]{0:T(128)} %item_ref.1, s32[16]{0:T(128)} %dest_ref.1, f32[1,256]{1,0:T(1,128)} %bitcast.2, f32[1,256]{1,0:T(1,128)} %bitcast.3, bf16[256,1024]{1,0:T(8,128)(2,1)} %gate_b_ref.1, ...), custom_call_target="tpu_custom_call" | custom-call | tf_op jit(solution)/shard_map/layer/pallas_call | solution.py:744
  85.1 0.0 copy-done
  85.1 0.0 copy-done.1
  85.1 0.0 copy-done.2
  85.1 0.0 copy-done.3
  85.1 1.7 %divide_subtract_fusion = (f32[256,128]{1,0:T(8,128)}, f32[256,128]{1,0:T(8,128)}, f32[256,128]{1,0:T(8,128)}) fusion(f32[256,128]{1,0:T(8,128)S(1)} %copy-done, f32[256,128]{1,0:T(8,128)} %layer.1, bf16[256,128]{1,0:T(8,128)(2,1)S(1)} %copy-done.1, f32[256,128]{1,0:T(8,128)S(1)} %copy-done.2, f32[256,128]{1,0:T(8,128)S(1)} %copy-done.3), kind=kLoop, calls=%fused_computation.2 | loop fusion | flops 425984 | bytes 983040 | tf_op jit(solution)/shard_map/sub | solution.py:776
Async XLA Ops:
  0.6 84.4 %copy-start = (f32[256,128]{1,0:T(8,128)S(1)}, f32[256,128]{1,0:T(8,128)}, u32[]{:S(2)}) copy-start(f32[256,128]{1,0:T(8,128)} %rows_hbm.1) | copy-start | bytes 393220
  0.6 84.4 %copy-start.1 = (bf16[256,128]{1,0:T(8,128)(2,1)S(1)}, bf16[256,128]{1,0:T(8,128)(2,1)}, u32[]{:S(2)}) copy-start(bf16[256,128]{1,0:T(8,128)(2,1)} %cot_hbm.1) | copy-start | bytes 196612
  0.7 84.4 %copy-start.2 = (f32[256,128]{1,0:T(8,128)S(1)}, f32[256,128]{1,0:T(8,128)}, u32[]{:S(2)}) copy-start(f32[256,128]{1,0:T(8,128)} %param.16) | copy-start | bytes 393220
  0.7 84.4 %copy-start.3 = (f32[256,128]{1,0:T(8,128)S(1)}, f32[256,128]{1,0:T(8,128)}, u32[]{:S(2)}) copy-start(f32[256,128]{1,0:T(8,128)} %param.17) | copy-start | bytes 393220

commit v5 on v4

--- a/solution.py
+++ b/solution.py
@@ -88,7 +88,7 @@
         "cot_send": dma,
         "cot_recv": dma,
         "owner_in": pltpu.VMEM((2, PARTS, OWN, HALF), BF),
-        "item_in": pltpu.VMEM((PARTS, BLOCK, HALF), BF),
+        "item_in": pltpu.VMEM((2, PARTS, BLOCK // 2, HALF), BF),
         "words_send": dma,
         "words_recv": dma,
         "rows_send": dma,
@@ -98,8 +98,8 @@
         "block_send": dma((2,)),
         "block_recv": dma((2, PLANE)),
         "item_send": dma,
-        "item_recv": dma,
-        "grad_send": dma,
+        "item_recv": dma((2,)),
+        "grad_send": dma((2,)),
         "grad_recv": dma((PLANE,)),
         "back_send": dma,
         "back_recv": dma,
@@ -400,13 +400,13 @@
             mode.spread[member] = dot(mat, to_columns).astype(BF)
             mode.collect[member] = dot_nt(from_tiles, mat).astype(BF)
 
-        def unpack_pair(n, carry):
-            for i in range(2):
-                unpack(2 * n + i)
+        def unpack_some(n, carry):
+            for i in range(4):
+                unpack(4 * n + i)
             return carry
 
         arrived(mode.words_in.at[: mode.members - 1], words_recv)
-        lax.fori_loop(0, mode.members // 2, unpack_pair, 0)
+        lax.fori_loop(0, mode.members // 4, unpack_some, 0)
 
         tiles = TILE_DEV * mode.members
         about = mode.words_in[0, slots]
@@ -553,12 +553,12 @@
         total = total + dot(hidden, tall[0, h])
     send_blocks(0, total.astype(BF))
 
-    def item_copy(mode, member, to_core):
+    def item_copy(mode, member, to_core, part):
         return remote(
-            mode.item_out.at[0, 2 * member + to_core],
-            item_in.at[mode.first_item + mode.own_member],
+            mode.item_out.at[0, 2 * member + to_core, pl.ds(part * BLOCK // 2, BLOCK // 2)],
+            item_in.at[part, mode.first_item + mode.own_member],
             item_send,
-            item_recv,
+            item_recv.at[part],
             mode.item_shard(member),
             to_core,
         )
@@ -573,15 +573,22 @@
 
         def send(member):
             for to_core in range(2):
-                item_copy(mode, member, to_core).start()
+                item_copy(mode, member, to_core, 0).start()
 
         def send_own():
-            item_copy(mode, mode.own_member, 1 - mode.core).start()
+            item_copy(mode, mode.own_member, 1 - mode.core, 0).start()
+
+        def send_rest(member):
+            for to_core in range(2):
+                item_copy(mode, member, to_core, 1).start()
 
         ahead(mode.members, mode.own_member, 2, partials, send, send_own)
-        item_in[mode.first_item + mode.own_member] = mode.item_out[
-            0, 2 * mode.own_member + mode.core
-        ]
+        around(mode.members, mode.own_member, send_rest)
+        item_copy(mode, mode.own_member, 1 - mode.core, 1).start()
+        own_out = mode.item_out[0, 2 * mode.own_member + mode.core]
+        for part in range(2):
+            rows = slice(part * BLOCK // 2, (part + 1) * BLOCK // 2)
+            item_in[part, mode.first_item + mode.own_member] = own_out[rows, :]
 
     per_mode(send_items)
 
@@ -590,53 +597,60 @@
         sibling_weight(n).wait_recv()
     arrived(cot_whole.at[other], cot_recv)
     load_cot.wait()
-    arrived(item_in.at[: PARTS - 1], item_recv)
-    halves = []
-    for mode in modes:
-        summed = item_in[mode.first_item].astype(F32)
-        for member in range(1, mode.members):
-            summed = summed + item_in[mode.first_item + member].astype(F32)
-        halves.append(summed)
-    message = jnp.concatenate(halves, axis=1)
     cot_full = jnp.concatenate([cot_whole[0], cot_whole[1]], axis=1)
-    scale_item = rms_scale(message)
-    query = (message * scale_item * item_gain).astype(BF)
-    grad_query = jnp.zeros((BLOCK, D), F32)
-    for h in range(2):
-        gate_pre = dot(query, wide[2, h])
-        up_pre = dot(query, wide[3, h])
-        grad_hidden = dot_nt(cot_full, tall[1, h])
-        value, slope = silu_parts(gate_pre)
-        grad_up = (grad_hidden * value).astype(BF)
-        grad_gate = (grad_hidden * up_pre * slope).astype(BF)
-        grad_query = grad_query + dot_nt(grad_gate, wide[2, h]) + dot_nt(grad_up, wide[3, h])
-    inner = jnp.sum(item_gain * grad_query * message, axis=1, keepdims=True)
-    cubed = scale_item * scale_item * scale_item
-    grad_message = (scale_item * item_gain * grad_query - message * cubed * inner / D).astype(BF)
-
-    def grad_copy(mode, member):
+
+    def item_layer(part):
+        arrived(item_in.at[part, : PARTS - 1], item_recv.at[part])
+        halves = []
+        for mode in modes:
+            summed = item_in[part, mode.first_item].astype(F32)
+            for member in range(1, mode.members):
+                summed = summed + item_in[part, mode.first_item + member].astype(F32)
+            halves.append(summed)
+        message = jnp.concatenate(halves, axis=1)
+        cot = cot_full[part * BLOCK // 2 : (part + 1) * BLOCK // 2, :]
+        scale_item = rms_scale(message)
+        query = (message * scale_item * item_gain).astype(BF)
+        grad_query = jnp.zeros((BLOCK // 2, D), F32)
+        for h in range(2):
+            gate_pre = dot(query, wide[2, h])
+            up_pre = dot(query, wide[3, h])
+            grad_hidden = dot_nt(cot, tall[1, h])
+            value, slope = silu_parts(gate_pre)
+            grad_up = (grad_hidden * value).astype(BF)
+            grad_gate = (grad_hidden * up_pre * slope).astype(BF)
+            grad_query = grad_query + dot_nt(grad_gate, wide[2, h]) + dot_nt(grad_up, wide[3, h])
+        inner = jnp.sum(item_gain * grad_query * message, axis=1, keepdims=True)
+        cubed = scale_item * scale_item * scale_item
+        return (scale_item * item_gain * grad_query - message * cubed * inner / D).astype(BF)
+
+    def grad_copy(mode, member, part):
         return remote(
-            mode.grad_out,
-            mode.rows.at[1, mode.own_member, rows16(m * BLOCK, BLOCK)],
-            grad_send,
+            mode.grad_out.at[pl.ds(part * BLOCK // 2, BLOCK // 2)],
+            mode.rows.at[1, mode.own_member, rows16(m * BLOCK + part * BLOCK // 2, BLOCK // 2)],
+            grad_send.at[part],
             grad_recv.at[mode.own_member],
             mode.item_shard(member),
             mode.core,
         )
 
+    for part in range(2):
+        grad_message = item_layer(part)
+        for mode in modes:
+            rows = slice(part * BLOCK // 2, (part + 1) * BLOCK // 2)
+            mode.grad_out[rows, :] = grad_message[:, mode.core * HALF : (mode.core + 1) * HALF]
+        for mode in modes:
+
+            @pl.when(m != mode.core)
+            def _(mode=mode, part=part):
+                grad_copy(mode, mode.own_member, part).start()
+
+            around(
+                mode.members,
+                mode.own_member,
+                lambda member, mode=mode, part=part: grad_copy(mode, member, part).start(),
+            )
     for mode in modes:
-        mode.grad_out[...] = grad_message[:, mode.core * HALF : (mode.core + 1) * HALF]
-    for mode in modes:
-
-        @pl.when(m != mode.core)
-        def _(mode=mode):
-            grad_copy(mode, mode.own_member).start()
-
-        around(
-            mode.members,
-            mode.own_member,
-            lambda member, mode=mode: grad_copy(mode, member).start(),
-        )
 
         @pl.when(m == mode.core)
         def _(mode=mode):
@@ -705,7 +719,8 @@
         for phase in range(2):
             sent(mode.owner_out.at[phase, : 2 * mode.columns - 1], owner_send.at[phase])
             sent(owner_in.at[phase, : PARTS - 1], block_send.at[phase])
-        sent(item_in.at[: PARTS - 1], grad_send)
+        for part in range(2):
+            sent(item_in.at[part, : PARTS - 1], grad_send.at[part])
         arrived(mode.back_in.at[: mode.members - 1], back_recv)
         for block in range(2):
             back = mode.back_in[0, block].astype(F32)
@@ -743,7 +758,7 @@
     anywhere = pl.BlockSpec(memory_space=pltpu.HBM)
     back_items = pl.pallas_call(
         kernel,
-        out_shape=jax.ShapeDtypeStruct((2 * BLOCK, HALF), F32),
+        out_shape=pltpu.VMEM((2 * BLOCK, HALF), F32),
         in_specs=[anywhere] * 3 + [smem, smem, vmem, vmem] + [anywhere] * 6,
         out_specs=vmem,
         scratch_shapes=[

time: 87.1 us -> 83.7 us (0.961)
  Pallas kernels: 84.4 us -> 82.1 us
  other arithmetic: 1.69 us -> 0.79 us
    pallas_call x1, Pallas kernels: 84.4 us -> 82.1 us  [local(): pl.pallas_call(kernel, out_shape=pltpu.VMEM((2 * BLOCK, HALF), F32), in_s...]
    sub x1, other arithmetic: 1.69 us -> 0.79 us  [local(): item_rows - LEARNING_RATE * new_first / (jnp.sqrt(new_second) + ADAM_EPSI...]
where the time goes in v5:
time: 83.7 us; the launch traced here: 83.6 us
  Pallas kernels  82.1 us (98%)
    pallas_call x1, Pallas kernels, local(): pl.pallas_call(kernel, out_shape=pltpu.VMEM((2 * BLOCK, HALF), F32), in_s...  82.1 us

profile of v5, /device:TPU:1, one launch (start us, length us, event | category | flops | bytes accessed | tf_op | source)
XLA Modules:
  0.0 83.6 jit_solution(14688126439781433932)
XLA Ops:
  0.6 0.0 copy-start
  0.6 0.0 copy-start.1
  0.7 0.0 copy-start.2
  0.7 0.0 copy-start.3
  0.7 82.1 %layer.1 = f32[256,128]{1,0:T(8,128)S(1)} custom-call(f32[256,128]{1,0:T(8,128)} %rows_hbm.1, bf16[256,128]{1,0:T(8,128)(2,1)} %cot_hbm.1, s32[16,8,128]{2,1,0:T(8,128)} %bits_hbm.1, s32[16]{0:T(128)} %item_ref.1, s32[16]{0:T(128)} %dest_ref.1, f32[1,256]{1,0:T(1,128)} %bitcast.2, f32[1,256]{1,0:T(1,128)} %bitcast.3, bf16[256,1024]{1,0:T(8,128)(2,1)} %gate_b_ref.1, ...), custom_call_target="tpu_custom_call" | custom-call | tf_op jit(solution)/shard_map/layer/pallas_call | solution.py:759
  82.8 0.0 copy-done
  82.8 0.0 copy-done.1
  82.8 0.0 copy-done.2
  82.8 0.0 copy-done.3
  82.8 0.8 divide_subtract_fusion
Async XLA Ops:
  0.6 82.2 %copy-start = (f32[256,128]{1,0:T(8,128)S(1)}, f32[256,128]{1,0:T(8,128)}, u32[]{:S(2)}) copy-start(f32[256,128]{1,0:T(8,128)} %rows_hbm.1) | copy-start | bytes 393220
  0.6 82.2 %copy-start.1 = (bf16[256,128]{1,0:T(8,128)(2,1)S(1)}, bf16[256,128]{1,0:T(8,128)(2,1)}, u32[]{:S(2)}) copy-start(bf16[256,128]{1,0:T(8,128)(2,1)} %cot_hbm.1) | copy-start | bytes 196612
  0.7 82.2 %copy-start.2 = (f32[256,128]{1,0:T(8,128)S(1)}, f32[256,128]{1,0:T(8,128)}, u32[]{:S(2)}) copy-start(f32[256,128]{1,0:T(8,128)} %param.16) | copy-start | bytes 393220
  0.7 82.2 %copy-start.3 = (f32[256,128]{1,0:T(8,128)S(1)}, f32[256,128]{1,0:T(8,128)}, u32[]{:S(2)}) copy-start(f32[256,128]{1,0:T(8,128)} %param.17) | copy-start | bytes 393220

commit v6 on v5

--- a/solution.py
+++ b/solution.py
@@ -81,10 +81,14 @@
         "sum_keep": pltpu.VMEM((OWN, D), F32),
         "item_rows": pltpu.VMEM((2 * BLOCK, HALF), F32),
         "tile_bits": pltpu.VMEM((TILE_DEV, 8, 128), jnp.int32),
-        "load_sem": dma((3,)),
-        "weight_own": dma((6,)),
-        "weight_send": dma((6,)),
-        "weight_recv": dma((6,)),
+        "tile_item": pltpu.SMEM((TILE_DEV,), jnp.int32),
+        "tile_dest": pltpu.SMEM((TILE_DEV,), jnp.int32),
+        "basket_gain": pltpu.VMEM((1, D), F32),
+        "item_gain": pltpu.VMEM((1, D), F32),
+        "load_sem": dma((7,)),
+        "weight_own": dma((2,)),
+        "weight_send": dma,
+        "weight_recv": dma((2,)),
         "cot_send": dma,
         "cot_recv": dma,
         "owner_in": pltpu.VMEM((2, PARTS, OWN, HALF), BF),
@@ -92,15 +96,15 @@
         "words_send": dma,
         "words_recv": dma,
         "rows_send": dma,
-        "rows_recv": dma((PLANE,)),
+        "rows_recv": dma((PLANE // 2,)),
         "owner_send": dma((2,)),
         "owner_recv": dma((2,)),
         "block_send": dma((2,)),
-        "block_recv": dma((2, PLANE)),
+        "block_recv": dma((2, PLANE // 4)),
         "item_send": dma,
         "item_recv": dma((2,)),
         "grad_send": dma((2,)),
-        "grad_recv": dma((PLANE,)),
+        "grad_recv": dma((PLANE // 2,)),
         "back_send": dma,
         "back_recv": dma,
     }
@@ -127,10 +131,10 @@
     rows_hbm,
     cot_hbm,
     bits_hbm,
-    item_ref,
-    dest_ref,
-    gain_b_ref,
-    gain_i_ref,
+    item_hbm,
+    dest_hbm,
+    gain_b_hbm,
+    gain_i_hbm,
     gate_b_ref,
     up_b_ref,
     down_b_ref,
@@ -203,13 +207,16 @@
         lax.fori_loop(0, count // size - 1, step, 0)
         group(count // size - 1, True)
 
-    def behind(count, own, size, wait_own, wait, work):
+    def turn_at(count, own, place, size):
+        return lax.div(lax.rem(place - own + count, count), size)
+
+    def behind(count, own, size, wait_first, wait, work):
         def group(n, first):
             places = [lax.rem(own + count - n * size - i, count) for i in range(size)]
             if first:
-                wait_own()
-            for place in places[1:] if first else places:
-                wait(place)
+                wait_first()
+            else:
+                wait(n)
             work(places)
 
         def step(n, carry):
@@ -237,20 +244,30 @@
 
     def own_weight(n):
         src, dst = weights[n]
-        return pltpu.make_async_copy(src, dst.at[m], weight_own.at[n])
+        return pltpu.make_async_copy(src, dst.at[m], weight_own.at[n // 3])
 
     def sibling_weight(n):
         src, dst = weights[n]
-        return remote(src, dst.at[m], weight_send.at[n], weight_recv.at[n], shard, other)
-
+        return remote(src, dst.at[m], weight_send, weight_recv.at[n // 3], shard, other)
+
+    item_ref, dest_ref = common["tile_item"], common["tile_dest"]
+    gain_b_ref, gain_i_ref = common["basket_gain"], common["item_gain"]
+    small_loads = [
+        pltpu.make_async_copy(src, dst, load_sem.at[3 + n])
+        for n, (src, dst) in enumerate(
+            (
+                (item_hbm, item_ref),
+                (dest_hbm, dest_ref),
+                (gain_b_hbm, gain_b_ref),
+                (gain_i_hbm, gain_i_ref),
+            )
+        )
+    ]
     load_rows = pltpu.make_async_copy(rows_hbm, rows_ref, load_sem.at[0])
     load_bits = pltpu.make_async_copy(bits_hbm, bits_ref, load_sem.at[1])
     load_cot = pltpu.make_async_copy(
         cot_hbm.at[rows16(m * BLOCK, BLOCK)], cot_whole.at[m], load_sem.at[2]
     )
-    load_rows.start()
-    load_bits.start()
-
     barrier = pltpu.get_barrier_semaphore()
 
     def greet(to_shard, to_core):
@@ -262,6 +279,10 @@
         for core in range(2):
             greet(z_to * PLANE + q, core)
 
+    load_rows.start()
+    load_bits.start()
+    for load in small_loads:
+        load.start()
     around(RING, z, greet_ring)
     around(2 * PLANE, me, lambda k: greet(z * PLANE + lax.div(k, 2), lax.rem(k, 2)))
     load_cot.start()
@@ -313,6 +334,8 @@
 
     load_rows.wait()
     load_bits.wait()
+    for load in small_loads:
+        load.wait()
     per_mode(prepare)
 
     pl.semaphore_wait(barrier, 2 * PLANE - 1 + 2 * (RING - 1))
@@ -332,7 +355,7 @@
             mode.rows.at[0, mode.own_member],
             mode.rows.at[0, mode.own_member],
             rows_send,
-            rows_recv.at[mode.own_member],
+            rows_recv.at[turn_at(mode.members, mode.own_member, member, 2)],
             mode.item_shard(member),
             mode.core,
         )
@@ -369,20 +392,38 @@
             mode.tile_sums[:, rows16(member * TILE_DEV, TILE_DEV), :] = high.reshape(shape)
             mode.tile_sums[:, rows16(tiles + member * TILE_DEV, TILE_DEV), :] = low.reshape(shape)
 
+    def turned(mode, tile_major, column_major):
+        same = (tile_major // mode.columns == column_major % TILE_DEV) & (
+            tile_major % mode.columns == column_major // TILE_DEV
+        )
+        return jnp.where(same, 1.0, 0.0).astype(BF)
+
+    def finish_selection(mode):
+        size = TILE_DEV * mode.columns
+        left = lax.broadcasted_iota(jnp.int32, (size, size), 0)
+        right = lax.broadcasted_iota(jnp.int32, (size, size), 1)
+        to_columns = turned(mode, left, right)
+
+        def turn_some(n, carry):
+            mats = [dot(mode.spread[4 * n + i], to_columns).astype(BF) for i in range(4)]
+            for i in range(4):
+                mode.spread[4 * n + i] = mats[i]
+            return carry
+
+        lax.fori_loop(0, mode.members // 4, turn_some, 0)
+        tiles = TILE_DEV * mode.members
+        eye_left = lax.broadcasted_iota(jnp.int32, (tiles, tiles), 0)
+        eye_right = lax.broadcasted_iota(jnp.int32, (tiles, tiles), 1)
+        eye = jnp.where(eye_left == eye_right, 1.0, 0.0).astype(BF)
+        mode.select_rows[...] = dot_nt(eye, mode.select_cols[:, :tiles]).astype(BF)
+
     def take_rows(mode):
         size = TILE_DEV * mode.columns
         slots = size // 128
         left = lax.broadcasted_iota(jnp.int32, (size, size), 0)
         right = lax.broadcasted_iota(jnp.int32, (size, size), 1)
 
-        def turn(tile_major, column_major):
-            same = (tile_major // mode.columns == column_major % TILE_DEV) & (
-                tile_major % mode.columns == column_major // TILE_DEV
-            )
-            return jnp.where(same, 1.0, 0.0).astype(BF)
-
-        to_columns = turn(left, right)
-        from_tiles = turn(right, left)
+        from_tiles = turned(mode, right, left)
         shifts = lax.broadcasted_iota(jnp.int32, (8, 16, 128), 1)
 
         def unpack(member):
@@ -397,7 +438,7 @@
                 parts = [jnp.where(item == block, bits, 0.0) for bits, item in halves]
                 blocks.append(parts[0] if slots == 1 else jnp.concatenate(parts, axis=1))
             mat = jnp.concatenate(blocks, axis=0).astype(BF)
-            mode.spread[member] = dot(mat, to_columns).astype(BF)
+            mode.spread[member] = mat
             mode.collect[member] = dot_nt(from_tiles, mat).astype(BF)
 
         def unpack_some(n, carry):
@@ -418,19 +459,12 @@
         block_of = lax.broadcasted_iota(jnp.int32, (BLOCK, tiles), 0)
         one_hot = jnp.where(block_of == all_dest, 1.0, 0.0).astype(BF)
         mode.select_cols[...] = jnp.concatenate([one_hot, one_hot], axis=1)
-        eye_left = lax.broadcasted_iota(jnp.int32, (tiles, tiles), 0)
-        eye_right = lax.broadcasted_iota(jnp.int32, (tiles, tiles), 1)
-        eye = jnp.where(eye_left == eye_right, 1.0, 0.0).astype(BF)
-        mode.select_rows[...] = lax.dot_general(
-            eye, one_hot, (((1,), (1,)), ((), ())), preferred_element_type=F32
-        ).astype(BF)
-
         behind(
             mode.members,
             mode.own_member,
             2,
-            lambda: None,
-            lambda member: arrived(mode.rows.at[0, member], rows_recv.at[member]),
+            lambda: arrived(mode.rows.at[0, 0], rows_recv.at[0]),
+            lambda n: arrived(mode.rows.at[0, :2], rows_recv.at[n]),
             lambda members: add_tiles(mode, 0, members),
         )
 
@@ -467,6 +501,8 @@
         owner_in[phase, mode.first + mode.own_column] = mode.owner_out[
             phase, 2 * mode.own_column + mode.core
         ]
+        if phase == 0:
+            finish_selection(mode)
 
     def sum_at_owners(phase):
         per_mode(lambda mode: send_sums(mode, phase))
@@ -484,7 +520,7 @@
             mode.block_out.at[phase],
             mode.block_in.at[phase, mode.own_column, rows16(m * OWN, OWN)],
             block_send.at[phase],
-            block_recv.at[phase, mode.own_column],
+            block_recv.at[phase, turn_at(mode.columns, mode.own_column, column, 4)],
             mode.basket_shard(column),
             mode.core,
         )
@@ -525,11 +561,8 @@
             mode.columns,
             mode.own_column,
             4,
-            lambda: arrived(
-                mode.block_in.at[phase, mode.own_column, :OWN],
-                block_recv.at[phase, mode.own_column],
-            ),
-            lambda column: arrived(mode.block_in.at[phase, column], block_recv.at[phase, column]),
+            lambda: arrived(owner_in.at[phase, :7], block_recv.at[phase, 0]),
+            lambda n: arrived(mode.block_in.at[phase, :4], block_recv.at[phase, n]),
             pick,
         )
 
@@ -538,9 +571,9 @@
 
     basket_sum = sum_at_owners(0)
     sum_keep[...] = basket_sum
-    for n in range(3):
-        own_weight(n).wait()
-        sibling_weight(n).wait_recv()
+    three = wide.at[:3, 0]
+    pltpu.make_async_copy(three, three, weight_own.at[0]).wait()
+    arrived(three, weight_recv.at[0])
     normed = basket_sum * rms_scale(basket_sum) * basket_gain
     normed_bf = normed.astype(BF)
     total = normed
@@ -592,9 +625,8 @@
 
     per_mode(send_items)
 
-    for n in range(3, 6):
-        own_weight(n).wait()
-        sibling_weight(n).wait_recv()
+    pltpu.make_async_copy(three, three, weight_own.at[1]).wait()
+    arrived(three, weight_recv.at[1])
     arrived(cot_whole.at[other], cot_recv)
     load_cot.wait()
     cot_full = jnp.concatenate([cot_whole[0], cot_whole[1]], axis=1)
@@ -629,7 +661,7 @@
             mode.grad_out.at[pl.ds(part * BLOCK // 2, BLOCK // 2)],
             mode.rows.at[1, mode.own_member, rows16(m * BLOCK + part * BLOCK // 2, BLOCK // 2)],
             grad_send.at[part],
-            grad_recv.at[mode.own_member],
+            grad_recv.at[turn_at(mode.members, mode.own_member, member, 2)],
             mode.item_shard(member),
             mode.core,
         )
@@ -662,10 +694,8 @@
             mode.members,
             mode.own_member,
             2,
-            lambda: arrived(
-                mode.rows.at[1, mode.own_member, :BLOCK], grad_recv.at[mode.own_member]
-            ),
-            lambda member: arrived(mode.rows.at[1, member], grad_recv.at[member]),
+            lambda: arrived(mode.item_out.at[0, :3], grad_recv.at[0]),
+            lambda n: arrived(mode.rows.at[1, :2], grad_recv.at[n]),
             lambda members: add_tiles(mode, 1, members),
         )
 
@@ -731,8 +761,7 @@
 
     per_mode(finish)
 
-    for n in range(6):
-        sibling_weight(n).wait_send()
+    sent(wide.at[:3], weight_send)
     cot_copy().wait_send()
 
 
@@ -754,12 +783,11 @@
     down_item,
 ):
     vmem = pl.BlockSpec(memory_space=pltpu.VMEM)
-    smem = pl.BlockSpec(memory_space=pltpu.SMEM)
     anywhere = pl.BlockSpec(memory_space=pltpu.HBM)
     back_items = pl.pallas_call(
         kernel,
         out_shape=pltpu.VMEM((2 * BLOCK, HALF), F32),
-        in_specs=[anywhere] * 3 + [smem, smem, vmem, vmem] + [anywhere] * 6,
+        in_specs=[anywhere] * 13,
         out_specs=vmem,
         scratch_shapes=[
             common_scratch(),

time: 83.7 us -> 82.5 us (0.986)
  Pallas kernels: 82.1 us -> 80.9 us
    pallas_call x1, Pallas kernels: 82.1 us -> 80.9 us  [local(): pl.pallas_call(kernel, out_shape=pltpu.VMEM((2 * BLOCK, HALF), F32), in_s...]
where the time goes in v6:
time: 82.5 us; the launch traced here: 82.4 us
  Pallas kernels  80.9 us (98%)
    pallas_call x1, Pallas kernels, local(): pl.pallas_call(kernel, out_shape=pltpu.VMEM((2 * BLOCK, HALF), F32), in_s...  80.9 us

profile of v6, /device:TPU:1, one launch (start us, length us, event | category | flops | bytes accessed | tf_op | source)
XLA Modules:
  0.0 82.4 jit_solution(18086416705810247531)
XLA Ops:
  0.6 0.0 copy-start
  0.6 0.0 copy-start.1
  0.7 0.0 copy-start.2
  0.7 0.0 copy-start.3
  0.7 80.9 %layer.1 = f32[256,128]{1,0:T(8,128)S(1)} custom-call(f32[256,128]{1,0:T(8,128)} %rows_hbm.1, bf16[256,128]{1,0:T(8,128)(2,1)} %cot_hbm.1, s32[16,8,128]{2,1,0:T(8,128)} %bits_hbm.1, s32[16]{0:T(128)} %item_hbm.1, s32[16]{0:T(128)} %dest_hbm.1, f32[1,256]{1,0:T(1,128)} %bitcast.2, f32[1,256]{1,0:T(1,128)} %bitcast.3, bf16[256,1024]{1,0:T(8,128)(2,1)} %gate_b_ref.1, ...), custom_call_target="tpu_custom_call" | custom-call | tf_op jit(solution)/shard_map/layer/pallas_call | solution.py:787
  81.6 0.0 copy-done
  81.6 0.0 copy-done.1
  81.6 0.0 copy-done.2
  81.6 0.0 copy-done.3
  81.6 0.8 divide_subtract_fusion
Async XLA Ops:
  0.6 81.0 %copy-start = (f32[256,128]{1,0:T(8,128)S(1)}, f32[256,128]{1,0:T(8,128)}, u32[]{:S(2)}) copy-start(f32[256,128]{1,0:T(8,128)} %rows_hbm.1) | copy-start | bytes 393220
  0.6 81.0 %copy-start.1 = (bf16[256,128]{1,0:T(8,128)(2,1)S(1)}, bf16[256,128]{1,0:T(8,128)(2,1)}, u32[]{:S(2)}) copy-start(bf16[256,128]{1,0:T(8,128)(2,1)} %cot_hbm.1) | copy-start | bytes 196612
  0.7 81.0 %copy-start.2 = (f32[256,128]{1,0:T(8,128)S(1)}, f32[256,128]{1,0:T(8,128)}, u32[]{:S(2)}) copy-start(f32[256,128]{1,0:T(8,128)} %param.16) | copy-start | bytes 393220
  0.7 81.0 %copy-start.3 = (f32[256,128]{1,0:T(8,128)S(1)}, f32[256,128]{1,0:T(8,128)}, u32[]{:S(2)}) copy-start(f32[256,128]{1,0:T(8,128)} %param.17) | copy-start | bytes 393220

commit v7 on v6

--- a/solution.py
+++ b/solution.py
@@ -13,6 +13,7 @@
 PLANE = 16
 PARTS = RING + PLANE
 OWN = 64
+PART = OWN // 2
 HIDDEN = 1024
 
 NORM_EPSILON = 1e-05
@@ -76,9 +77,9 @@
         "wide": pltpu.VMEM((4, 2, D, HIDDEN), BF),
         "tall": pltpu.VMEM((2, 2, HIDDEN, D), BF),
         "cot_whole": pltpu.VMEM((2, BLOCK, HALF), BF),
-        "gate_keep": pltpu.VMEM((2, OWN, HIDDEN), F32),
-        "up_keep": pltpu.VMEM((2, OWN, HIDDEN), F32),
-        "sum_keep": pltpu.VMEM((OWN, D), F32),
+        "gate_keep": pltpu.VMEM((2, 2, PART, HIDDEN), F32),
+        "up_keep": pltpu.VMEM((2, 2, PART, HIDDEN), F32),
+        "sum_keep": pltpu.VMEM((2, PART, D), F32),
         "item_rows": pltpu.VMEM((2 * BLOCK, HALF), F32),
         "tile_bits": pltpu.VMEM((TILE_DEV, 8, 128), jnp.int32),
         "tile_item": pltpu.SMEM((TILE_DEV,), jnp.int32),
@@ -91,15 +92,15 @@
         "weight_recv": dma((2,)),
         "cot_send": dma,
         "cot_recv": dma,
-        "owner_in": pltpu.VMEM((2, PARTS, OWN, HALF), BF),
+        "owner_in": pltpu.VMEM((2, 2, PARTS, PART, HALF), BF),
         "item_in": pltpu.VMEM((2, PARTS, BLOCK // 2, HALF), BF),
         "words_send": dma,
         "words_recv": dma,
         "rows_send": dma,
         "rows_recv": dma((PLANE // 2,)),
         "owner_send": dma((2,)),
-        "owner_recv": dma((2,)),
-        "block_send": dma((2,)),
+        "owner_recv": dma((2, 2)),
+        "block_send": dma((2, 2)),
         "block_recv": dma((2, PLANE // 4)),
         "item_send": dma,
         "item_recv": dma((2,)),
@@ -470,12 +471,12 @@
 
     per_mode(take_rows)
 
-    def owner_copy(mode, phase, column, to_core):
+    def owner_copy(mode, phase, column, to_core, part):
         return remote(
-            mode.owner_out.at[phase, 2 * column + to_core],
-            owner_in.at[phase, mode.first + mode.own_column],
+            mode.owner_out.at[phase, 2 * column + to_core, pl.ds(part * PART, PART)],
+            owner_in.at[phase, part, mode.first + mode.own_column],
             owner_send.at[phase],
-            owner_recv.at[phase],
+            owner_recv.at[phase, part],
             mode.basket_shard(column),
             to_core,
         )
@@ -492,58 +493,67 @@
 
         def send(column):
             for to_core in range(2):
-                owner_copy(mode, phase, column, to_core).start()
+                owner_copy(mode, phase, column, to_core, 0).start()
 
         def send_own():
-            owner_copy(mode, phase, mode.own_column, 1 - mode.core).start()
+            owner_copy(mode, phase, mode.own_column, 1 - mode.core, 0).start()
+
+        def send_rest(column):
+            for to_core in range(2):
+                owner_copy(mode, phase, column, to_core, 1).start()
 
         ahead(mode.columns, mode.own_column, 4, column_sums, send, send_own)
-        owner_in[phase, mode.first + mode.own_column] = mode.owner_out[
-            phase, 2 * mode.own_column + mode.core
-        ]
+        around(mode.columns, mode.own_column, send_rest)
+        owner_copy(mode, phase, mode.own_column, 1 - mode.core, 1).start()
+        own_out = mode.owner_out[phase, 2 * mode.own_column + mode.core]
+        for part in range(2):
+            rows = slice(part * PART, (part + 1) * PART)
+            owner_in[phase, part, mode.first + mode.own_column] = own_out[rows, :]
         if phase == 0:
             finish_selection(mode)
 
-    def sum_at_owners(phase):
-        per_mode(lambda mode: send_sums(mode, phase))
-        arrived(owner_in.at[phase, : PARTS - 1], owner_recv.at[phase])
+    def sum_at_owners(phase, part):
+        arrived(owner_in.at[phase, part, : PARTS - 1], owner_recv.at[phase, part])
         halves = []
         for mode in modes:
-            total = owner_in[phase, mode.first].astype(F32)
+            total = owner_in[phase, part, mode.first].astype(F32)
             for column in range(1, mode.columns):
-                total = total + owner_in[phase, mode.first + column].astype(F32)
+                total = total + owner_in[phase, part, mode.first + column].astype(F32)
             halves.append(total)
         return jnp.concatenate(halves, axis=1)
 
-    def block_copy(mode, phase, column):
+    def block_copy(mode, phase, column, part):
         return remote(
-            mode.block_out.at[phase],
-            mode.block_in.at[phase, mode.own_column, rows16(m * OWN, OWN)],
-            block_send.at[phase],
+            mode.block_out.at[phase, pl.ds(part * PART, PART)],
+            mode.block_in.at[phase, mode.own_column, rows16(m * OWN + part * PART, PART)],
+            block_send.at[phase, part],
             block_recv.at[phase, turn_at(mode.columns, mode.own_column, column, 4)],
             mode.basket_shard(column),
             mode.core,
         )
 
-    def send_blocks(phase, values):
+    def send_blocks(phase, part, values):
         for mode in modes:
-            mode.block_out[phase] = values[:, mode.core * HALF : (mode.core + 1) * HALF]
+            rows = slice(part * PART, (part + 1) * PART)
+            mode.block_out[phase, rows, :] = values[:, mode.core * HALF : (mode.core + 1) * HALF]
         for mode in modes:
 
             @pl.when(m != mode.core)
             def _(mode=mode):
-                block_copy(mode, phase, mode.own_column).start()
+                block_copy(mode, phase, mode.own_column, part).start()
 
             around(
                 mode.columns,
                 mode.own_column,
-                lambda column, mode=mode: block_copy(mode, phase, column).start(),
+                lambda column, mode=mode: block_copy(mode, phase, column, part).start(),
             )
 
             @pl.when(m == mode.core)
             def _(mode=mode):
-                place = slice(mode.core * OWN, (mode.core + 1) * OWN)
-                mode.block_in[phase, mode.own_column, place, :] = mode.block_out[phase]
+                start = mode.core * OWN + part * PART
+                mode.block_in[phase, mode.own_column, start : start + PART, :] = mode.block_out[
+                    phase, part * PART : (part + 1) * PART
+                ]
 
     def pick_all(mode, phase):
         def pick(columns):
@@ -561,7 +571,7 @@
             mode.columns,
             mode.own_column,
             4,
-            lambda: arrived(owner_in.at[phase, :7], block_recv.at[phase, 0]),
+            lambda: arrived(owner_in.at[phase, 0, :14], block_recv.at[phase, 0]),
             lambda n: arrived(mode.block_in.at[phase, :4], block_recv.at[phase, n]),
             pick,
         )
@@ -569,22 +579,29 @@
     basket_gain = gain_b_ref[...]
     item_gain = gain_i_ref[...]
 
-    basket_sum = sum_at_owners(0)
-    sum_keep[...] = basket_sum
     three = wide.at[:3, 0]
-    pltpu.make_async_copy(three, three, weight_own.at[0]).wait()
-    arrived(three, weight_recv.at[0])
-    normed = basket_sum * rms_scale(basket_sum) * basket_gain
-    normed_bf = normed.astype(BF)
-    total = normed
-    for h in range(2):
-        gate_pre = dot(normed_bf, wide[0, h])
-        up_pre = dot(normed_bf, wide[1, h])
-        gate_keep[h] = gate_pre
-        up_keep[h] = up_pre
-        hidden = (gate_pre * jax.nn.sigmoid(gate_pre) * up_pre).astype(BF)
-        total = total + dot(hidden, tall[0, h])
-    send_blocks(0, total.astype(BF))
+    per_mode(lambda mode: send_sums(mode, 0))
+
+    def basket_layer(part):
+        basket_sum = sum_at_owners(0, part)
+        sum_keep[part] = basket_sum
+        if part == 0:
+            pltpu.make_async_copy(three, three, weight_own.at[0]).wait()
+            arrived(three, weight_recv.at[0])
+        normed = basket_sum * rms_scale(basket_sum) * basket_gain
+        normed_bf = normed.astype(BF)
+        total = normed
+        for h in range(2):
+            gate_pre = dot(normed_bf, wide[0, h])
+            up_pre = dot(normed_bf, wide[1, h])
+            gate_keep[part, h] = gate_pre
+            up_keep[part, h] = up_pre
+            hidden = (gate_pre * jax.nn.sigmoid(gate_pre) * up_pre).astype(BF)
+            total = total + dot(hidden, tall[0, h])
+        send_blocks(0, part, total.astype(BF))
+
+    for part in range(2):
+        basket_layer(part)
 
     def item_copy(mode, member, to_core, part):
         return remote(
@@ -700,21 +717,29 @@
         )
 
     per_mode(take_grads)
-    grad_out = sum_at_owners(1)
-    grad_out_bf = grad_out.astype(BF)
-    grad_normed = grad_out
-    for h in range(2):
-        grad_hidden = dot_nt(grad_out_bf, tall[0, h])
-        value, slope = silu_parts(gate_keep[h])
-        grad_up = (grad_hidden * value).astype(BF)
-        grad_gate = (grad_hidden * up_keep[h] * slope).astype(BF)
-        grad_normed = grad_normed + (dot_nt(grad_gate, wide[0, h]) + dot_nt(grad_up, wide[1, h]))
-    sums = sum_keep[...]
-    scale_basket = rms_scale(sums)
-    inner_basket = jnp.sum(basket_gain * grad_normed * sums, axis=1, keepdims=True)
-    cubed_basket = scale_basket * scale_basket * scale_basket
-    grad_sum = scale_basket * basket_gain * grad_normed - sums * cubed_basket * inner_basket / D
-    send_blocks(1, grad_sum.astype(BF))
+    per_mode(lambda mode: send_sums(mode, 1))
+
+    def basket_backward(part):
+        grad_out = sum_at_owners(1, part)
+        grad_out_bf = grad_out.astype(BF)
+        grad_normed = grad_out
+        for h in range(2):
+            grad_hidden = dot_nt(grad_out_bf, tall[0, h])
+            value, slope = silu_parts(gate_keep[part, h])
+            grad_up = (grad_hidden * value).astype(BF)
+            grad_gate = (grad_hidden * up_keep[part, h] * slope).astype(BF)
+            grad_normed = grad_normed + (
+                dot_nt(grad_gate, wide[0, h]) + dot_nt(grad_up, wide[1, h])
+            )
+        sums = sum_keep[part]
+        scale_basket = rms_scale(sums)
+        inner_basket = jnp.sum(basket_gain * grad_normed * sums, axis=1, keepdims=True)
+        cubed_basket = scale_basket * scale_basket * scale_basket
+        grad_sum = scale_basket * basket_gain * grad_normed - sums * cubed_basket * inner_basket / D
+        send_blocks(1, part, grad_sum.astype(BF))
+
+    for part in range(2):
+        basket_backward(part)
 
     def back_copy(mode, member):
         return remote(
@@ -748,7 +773,8 @@
         sent(mode.item_out.at[0, : 2 * mode.members - 1], item_send)
         for phase in range(2):
             sent(mode.owner_out.at[phase, : 2 * mode.columns - 1], owner_send.at[phase])
-            sent(owner_in.at[phase, : PARTS - 1], block_send.at[phase])
+            for part in range(2):
+                sent(owner_in.at[phase, part, : PARTS - 1], block_send.at[phase, part])
         for part in range(2):
             sent(item_in.at[part, : PARTS - 1], grad_send.at[part])
         arrived(mode.back_in.at[: mode.members - 1], back_recv)

time: 82.5 us -> 81.6 us (0.989)
  Pallas kernels: 80.9 us -> 80 us
    pallas_call x1, Pallas kernels: 80.9 us -> 80 us  [local(): pl.pallas_call(kernel, out_shape=pltpu.VMEM((2 * BLOCK, HALF), F32), in_s...]
where the time goes in v7:
time: 81.6 us; the launch traced here: 81.5 us
  Pallas kernels  80 us (98%)
    pallas_call x1, Pallas kernels, local(): pl.pallas_call(kernel, out_shape=pltpu.VMEM((2 * BLOCK, HALF), F32), in_s...  80 us

profile of v7, /device:TPU:1, one launch (start us, length us, event | category | flops | bytes accessed | tf_op | source)
XLA Modules:
  0.0 81.5 jit_solution(9304071977346861860)
XLA Ops:
  0.6 0.0 copy-start
  0.6 0.0 copy-start.1
  0.7 0.0 copy-start.2
  0.7 0.0 copy-start.3
  0.7 80.0 %layer.1 = f32[256,128]{1,0:T(8,128)S(1)} custom-call(f32[256,128]{1,0:T(8,128)} %rows_hbm.1, bf16[256,128]{1,0:T(8,128)(2,1)} %cot_hbm.1, s32[16,8,128]{2,1,0:T(8,128)} %bits_hbm.1, s32[16]{0:T(128)} %item_hbm.1, s32[16]{0:T(128)} %dest_hbm.1, f32[1,256]{1,0:T(1,128)} %bitcast.2, f32[1,256]{1,0:T(1,128)} %bitcast.3, bf16[256,1024]{1,0:T(8,128)(2,1)} %gate_b_ref.1, ...), custom_call_target="tpu_custom_call" | custom-call | tf_op jit(solution)/shard_map/layer/pallas_call | solution.py:813
  80.6 0.0 copy-done
  80.7 0.0 copy-done.1
  80.7 0.0 copy-done.2
  80.7 0.0 copy-done.3
  80.7 0.8 divide_subtract_fusion
Async XLA Ops:
  0.6 80.0 %copy-start = (f32[256,128]{1,0:T(8,128)S(1)}, f32[256,128]{1,0:T(8,128)}, u32[]{:S(2)}) copy-start(f32[256,128]{1,0:T(8,128)} %rows_hbm.1) | copy-start | bytes 393220
  0.6 80.0 %copy-start.1 = (bf16[256,128]{1,0:T(8,128)(2,1)S(1)}, bf16[256,128]{1,0:T(8,128)(2,1)}, u32[]{:S(2)}) copy-start(bf16[256,128]{1,0:T(8,128)(2,1)} %cot_hbm.1) | copy-start | bytes 196612
  0.7 80.0 %copy-start.2 = (f32[256,128]{1,0:T(8,128)S(1)}, f32[256,128]{1,0:T(8,128)}, u32[]{:S(2)}) copy-start(f32[256,128]{1,0:T(8,128)} %param.16) | copy-start | bytes 393220
  0.7 80.0 %copy-start.3 = (f32[256,128]{1,0:T(8,128)S(1)}, f32[256,128]{1,0:T(8,128)}, u32[]{:S(2)}) copy-start(f32[256,128]{1,0:T(8,128)} %param.17) | copy-start | bytes 393220

commit v8 on v7

--- a/solution.py
+++ b/solution.py
@@ -632,7 +632,7 @@
             for to_core in range(2):
                 item_copy(mode, member, to_core, 1).start()
 
-        ahead(mode.members, mode.own_member, 2, partials, send, send_own)
+        ahead(mode.members, mode.own_member, 4, partials, send, send_own)
         around(mode.members, mode.own_member, send_rest)
         item_copy(mode, mode.own_member, 1 - mode.core, 1).start()
         own_out = mode.item_out[0, 2 * mode.own_member + mode.core]
@@ -762,7 +762,7 @@
         ahead(
             mode.members,
             mode.own_member,
-            2,
+            4,
             partials,
             lambda member: back_copy(mode, member).start(),
             lambda: None,

time: 81.6 us -> 81.6 us (level)
  no operation moved by 1% of the time
where the time goes in v8:
time: 81.6 us; the launch traced here: 81.5 us
  Pallas kernels  80 us (98%)
    pallas_call x1, Pallas kernels, local(): pl.pallas_call(kernel, out_shape=pltpu.VMEM((2 * BLOCK, HALF), F32), in_s...  80 us

profile of v8, /device:TPU:1, one launch (start us, length us, event | category | flops | bytes accessed | tf_op | source)
XLA Modules:
  0.0 81.5 jit_solution(15927071654860354170)
XLA Ops:
  0.6 0.0 copy-start
  0.6 0.0 copy-start.1
  0.7 0.0 copy-start.2
  0.7 0.0 copy-start.3
  0.7 80.0 %layer.1 = f32[256,128]{1,0:T(8,128)S(1)} custom-call(f32[256,128]{1,0:T(8,128)} %rows_hbm.1, bf16[256,128]{1,0:T(8,128)(2,1)} %cot_hbm.1, s32[16,8,128]{2,1,0:T(8,128)} %bits_hbm.1, s32[16]{0:T(128)} %item_hbm.1, s32[16]{0:T(128)} %dest_hbm.1, f32[1,256]{1,0:T(1,128)} %bitcast.2, f32[1,256]{1,0:T(1,128)} %bitcast.3, bf16[256,1024]{1,0:T(8,128)(2,1)} %gate_b_ref.1, ...), custom_call_target="tpu_custom_call" | custom-call | tf_op jit(solution)/shard_map/layer/pallas_call | solution.py:813
  80.7 0.0 copy-done
  80.7 0.0 copy-done.1
  80.7 0.0 copy-done.2
  80.7 0.0 copy-done.3
  80.7 0.8 divide_subtract_fusion
Async XLA Ops:
  0.6 80.1 %copy-start = (f32[256,128]{1,0:T(8,128)S(1)}, f32[256,128]{1,0:T(8,128)}, u32[]{:S(2)}) copy-start(f32[256,128]{1,0:T(8,128)} %rows_hbm.1) | copy-start | bytes 393220
  0.6 80.1 %copy-start.1 = (bf16[256,128]{1,0:T(8,128)(2,1)S(1)}, bf16[256,128]{1,0:T(8,128)(2,1)}, u32[]{:S(2)}) copy-start(bf16[256,128]{1,0:T(8,128)(2,1)} %cot_hbm.1) | copy-start | bytes 196612
  0.7 80.1 %copy-start.2 = (f32[256,128]{1,0:T(8,128)S(1)}, f32[256,128]{1,0:T(8,128)}, u32[]{:S(2)}) copy-start(f32[256,128]{1,0:T(8,128)} %param.16) | copy-start | bytes 393220
  0.7 80.1 %copy-start.3 = (f32[256,128]{1,0:T(8,128)S(1)}, f32[256,128]{1,0:T(8,128)}, u32[]{:S(2)}) copy-start(f32[256,128]{1,0:T(8,128)} %param.17) | copy-start | bytes 393220
